TPU v7x, 32 devices: a whole 2x2x4 slice. The times are simulated.
32 devices in a mesh: lon: 8 (over y, x, core), lat: 4 (over z).
Axes of the slice: x: 2, y: 2, z: 4, core: 2. Of those that a mesh axis runs over, the one named last changes fastest.
Arguments:
- ocean_state: float32 [3, 8, 64, 1024], P(None, None, 'lat', 'lon'), may hold values from -6 to 6
- diffusivity: float32 [8, 64, 1024], P(None, 'lat', 'lon'), may hold values from 0.02 to 0.22
- depth_levels: int32 [64, 1024], P('lat', 'lon'), may hold values from 0 to 8, as said below
- fold_pair: int32 [1024], replicated, may hold values from 0 to 1023, as said below
- first_weight: bfloat16 [9, 64, 24], replicated, may hold values from -0.4375 to 0.4375
- mix_weight: bfloat16 [64, 64], replicated, may hold values from -0.75 to 0.75
- last_weight: bfloat16 [9, 16, 64], replicated, may hold values from -0.25 to 0.25
- cotangent: bfloat16 [16, 64, 1024], P(None, 'lat', 'lon'), may hold values from -6 to 6
- active_index: int32 [8192], replicated, may hold values from 0 to 27135, as said below
Outputs:
- new_state: float32 [3, 8, 64, 1024], P(None, None, 'lat', 'lon')
- closure: bfloat16 [16, 64, 1024], P(None, 'lat', 'lon')
- grad_active: float32 [8192], replicated
Inputs may be any that keep to these rules, and one draw needn't show every extreme that they name: `depth_levels`: 0 marks land; otherwise the number of wet levels of the column. fold_pair[i] = (s - i) mod 1024 for one s, the same for every i. `active_index`: distinct entries; 0 and 27135 are always among them.
All inputs are finite; a program needn't handle non-finite values.
Results may differ from a plain program's by a relative error of at most 0.0065.
Values may be sent and summed in bfloat16 or wider, within the bound.
A program may use at most 64 MiB of HBM per device.

v0:
```python
import math

import jax
import jax.numpy as jnp
from jax import lax
from jax.sharding import PartitionSpec as P

coriolis_peak = 0.25
pressure_scale = 0.05
advect_scale = 0.25


def padded_2(cells, sides, width):
    for axis, dim in sides:
        count = lax.axis_size(axis)
        head = lax.slice_in_dim(cells, 0, width, axis=dim)
        tail = lax.slice_in_dim(cells, cells.shape[dim] - width, cells.shape[dim], axis=dim)
        cells = jnp.concatenate(
            [
                lax.ppermute(tail, axis, [(i, (i + 1) % count) for i in range(count)]),
                cells,
                lax.ppermute(head, axis, [((i + 1) % count, i) for i in range(count)]),
            ],
            axis=dim,
        )
    return cells


def coriolis(row_ids, row_total):
    mirrored = jnp.where(row_ids >= row_total, 2 * row_total - 1 - row_ids, row_ids)
    return coriolis_peak * jnp.sin(
        math.pi * (mirrored.astype(jnp.float32) + 0.5) / row_total - 0.5 * math.pi
    )


def offset_view(field, shift_row, shift_col):
    height = field.shape[1] - 2
    width = field.shape[2] - 2
    return field[:, 1 + shift_row : 1 + shift_row + height, 1 + shift_col : 1 + shift_col + width]


def stencil(padded, coriolis_rows):
    u_all = padded[0]
    v_all = padded[1]
    t_all = padded[2]
    k_all = padded[3]
    k_center = offset_view(k_all, 0, 0)
    k_east = jnp.sqrt(k_center * offset_view(k_all, 0, 1))
    k_west = jnp.sqrt(k_center * offset_view(k_all, 0, -1))
    k_north = jnp.sqrt(k_center * offset_view(k_all, 1, 0))
    k_south = jnp.sqrt(k_center * offset_view(k_all, -1, 0))

    def diffuse(field):
        middle = offset_view(field, 0, 0)
        return (
            k_east * (offset_view(field, 0, 1) - middle)
            + k_west * (offset_view(field, 0, -1) - middle)
            + k_north * (offset_view(field, 1, 0) - middle)
            + k_south * (offset_view(field, -1, 0) - middle)
        )

    pressure = pressure_scale * jnp.cumsum(t_all, axis=0)
    wet_here = (k_center > 0).astype(jnp.float32)
    f_rows = coriolis_rows[None, :, None]
    u_mid = offset_view(u_all, 0, 0)
    v_mid = offset_view(v_all, 0, 0)
    t_mid = offset_view(t_all, 0, 0)
    u_change = f_rows * v_mid - 0.5 * (offset_view(pressure, 0, 1) - offset_view(pressure, 0, -1))
    v_change = -f_rows * u_mid - 0.5 * (offset_view(pressure, 1, 0) - offset_view(pressure, -1, 0))
    t_change = (
        -advect_scale
        * 0.5
        * (
            u_mid * (offset_view(t_all, 0, 1) - offset_view(t_all, 0, -1))
            + v_mid * (offset_view(t_all, 1, 0) - offset_view(t_all, -1, 0))
        )
    )
    return jnp.stack(
        [
            wet_here * (u_mid + u_change + diffuse(u_all)),
            wet_here * (v_mid + v_change + diffuse(v_all)),
            wet_here * (t_mid + t_change + diffuse(t_all)),
        ]
    )


def convolve(padded, weight):
    height = padded.shape[1] - 2
    width = padded.shape[2] - 2
    summed = None
    for tap_index in range(9):
        tap_row = tap_index // 3
        tap_col = tap_index % 3
        term = jnp.einsum(
            "oc,cyx->oyx",
            weight[tap_index],
            padded[:, tap_row : tap_row + height, tap_col : tap_col + width],
            preferred_element_type=jnp.float32,
        )
        summed = term if tap_index == 0 else summed + term
    return summed


def convolve_back(padded, weight):
    height = padded.shape[1] - 2
    width = padded.shape[2] - 2
    summed = None
    for tap_index in range(9):
        tap_row = tap_index // 3
        tap_col = tap_index % 3
        term = jnp.einsum(
            "oc,oyx->cyx",
            weight[tap_index],
            padded[:, 2 - tap_row : 2 - tap_row + height, 2 - tap_col : 2 - tap_col + width],
            preferred_element_type=jnp.float32,
        )
        summed = term if tap_index == 0 else summed + term
    return summed


def tap_grads(grad, padded):
    height = grad.shape[1]
    width = grad.shape[2]
    terms = []
    for tap_index in range(9):
        tap_row = tap_index // 3
        tap_col = tap_index % 3
        terms.append(
            jnp.einsum(
                "oyx,cyx->oc",
                grad,
                padded[:, tap_row : tap_row + height, tap_col : tap_col + width],
                preferred_element_type=jnp.float32,
            )
        )
    return jnp.stack(terms)


def silu_slope(pre):
    sigma = jax.nn.sigmoid(pre)
    return sigma * (1.0 + pre * (1.0 - sigma))


def on_device(
    ocean_state,
    diffusivity,
    depth_levels,
    fold_pair,
    first_weight,
    mix_weight,
    last_weight,
    cotangent,
    active_index,
):
    depth_count = ocean_state.shape[1]
    row_count = ocean_state.shape[2]
    col_count = ocean_state.shape[3]
    lat_index = lax.axis_index("lat")
    lon_index = lax.axis_index("lon")
    row_total = row_count * lax.axis_size("lat")
    col_total = col_count * lax.axis_size("lon")
    at_top = lat_index == lax.axis_size("lat") - 1
    at_bottom = lat_index == 0
    first_row = lat_index * row_count
    level_ids = jnp.arange(depth_count, dtype=jnp.int32)
    wet_mask = (level_ids[:, None, None] < depth_levels[None]).astype(jnp.float32)
    wet_kappa = diffusivity * wet_mask
    fields = ocean_state * wet_mask[None]
    fold_signs = jnp.concatenate(
        [-jnp.ones((2 * depth_count,), jnp.float32), jnp.ones((2 * depth_count,), jnp.float32)]
    )
    own_rows = first_row + jnp.arange(row_count, dtype=jnp.int32)
    for step_index in range(2):
        source = jnp.concatenate([fields, wet_kappa[None]], axis=0).reshape(
            4 * depth_count, row_count, col_count
        )
        rim = padded_2(source, (("lon", 2), ("lat", 1)), 1)
        top_rows = lax.all_gather(source[:, row_count - 1 :, :], "lon", axis=2, tiled=True)
        col_ids = (
            lon_index * col_count - 1 + jnp.arange(col_count + 2 * 1, dtype=jnp.int32)
        ) % col_total
        partner = jnp.take(fold_pair, col_ids)
        north_rows = jnp.stack(
            [fold_signs[:, None] * jnp.take(top_rows[:, 1 - 1, :], partner, axis=1)], axis=1
        )
        close_height = rim.shape[1]
        close_upper = jnp.where(at_top, north_rows, rim[:, close_height - 1 :, :])
        close_lower = jnp.where(at_bottom, jnp.zeros_like(north_rows), rim[:, :1, :])
        padded = jnp.concatenate(
            [close_lower, rim[:, 1 : close_height - 1, :], close_upper], axis=1
        ).reshape(4, depth_count, row_count + 2, col_count + 2)
        fields = stencil(padded, coriolis(own_rows, row_total))

    def open_deep(rim, margin):
        height = rim.shape[1]
        upper = jnp.where(
            at_top, jnp.zeros_like(rim[:, height - margin :, :]), rim[:, height - margin :, :]
        )
        lower = jnp.where(at_bottom, jnp.zeros_like(rim[:, :margin, :]), rim[:, :margin, :])
        return jnp.concatenate([lower, rim[:, margin : height - margin, :], upper], axis=1)

    in_channels = 3 * depth_count
    inputs = fields.reshape(in_channels, row_count, col_count).astype(jnp.bfloat16)
    level_mask = jnp.concatenate([wet_mask, wet_mask], axis=0)
    grad_scale = 1.0 / math.sqrt(row_total * col_total)
    out_grad = (grad_scale * level_mask * cotangent.astype(jnp.float32)).astype(jnp.bfloat16)
    stacked_net = jnp.concatenate([inputs, out_grad], axis=0)
    joined = open_deep(padded_2(stacked_net, (("lon", 2), ("lat", 1)), 1), 1)
    x_rim = joined[:in_channels]
    g_rim = joined[in_channels:]
    pre_first = convolve(x_rim, first_weight)
    hidden_first = jax.nn.silu(pre_first).astype(jnp.bfloat16)
    pre_mix = jnp.einsum(
        "oc,cyx->oyx", mix_weight, hidden_first, preferred_element_type=jnp.float32
    )
    hidden_mix = jax.nn.silu(pre_mix).astype(jnp.bfloat16)
    h_rim = open_deep(padded_2(hidden_mix, (("lon", 2), ("lat", 1)), 1), 1)
    closure = (level_mask * convolve(h_rim, last_weight)).astype(jnp.bfloat16)
    grad_last = tap_grads(out_grad, h_rim)
    back_mix = convolve_back(g_rim, last_weight)
    delta_mix = (back_mix * silu_slope(pre_mix)).astype(jnp.bfloat16)
    grad_mix = jnp.einsum(
        "oyx,cyx->oc", delta_mix, hidden_first, preferred_element_type=jnp.float32
    )
    back_first = jnp.einsum(
        "oc,oyx->cyx", mix_weight, delta_mix, preferred_element_type=jnp.float32
    )
    delta_first = (back_first * silu_slope(pre_first)).astype(jnp.bfloat16)
    grad_first = tap_grads(delta_first, x_rim)
    flat = jnp.concatenate([grad_first.reshape(-1), grad_mix.reshape(-1), grad_last.reshape(-1)])
    grad_active = jnp.take(lax.psum(flat, ("lon", "lat")), active_index)
    return (fields, closure, grad_active)


def solution(mesh):
    in_specs = (
        P(None, None, "lat", "lon"),
        P(None, "lat", "lon"),
        P("lat", "lon"),
        P(),
        P(),
        P(),
        P(),
        P(None, "lat", "lon"),
        P(),
    )
    out_specs = (P(None, None, "lat", "lon"), P(None, "lat", "lon"), P())
    return jax.shard_map(
        on_device, mesh=mesh, in_specs=in_specs, out_specs=out_specs, check_vma=False
    )
```

profile of v0, /device:TPU:0, one launch (start us, length us, event | category | flops | bytes accessed | tf_op | source)
XLA Modules:
  0.0 267.3 jit_solution(14765382128265965478)
XLA Ops:
  7.2 0.7 fusion.150
  7.9 0.9 fusion.227
  8.8 1.0 copy_multiply_fusion
  10.0 0.5 collective-permute-start
  10.5 2.9 %collective-permute-start.1 = (f32[32,16,1]{2,0,1:T(8,128)S(1)}, f32[32,16,1]{2,0,1:T(8,128)S(1)}, u32[]{:S(2)}, u32[]{:S(2)}) collective-permute-start(f32[32,16,1]{2,0,1:T(8,128)S(1)} %get-tuple-element.32), channel_id=1, source_target_pairs={{4,0},{8,4},{12,8},{16,12},{20,16},{24,20},{28,24},{0,28},{5,1},{9... | collective-permute-start | bytes 6152 | tf_op jit(solution)/shard_map/ppermute | solution.py:22
  13.5 1.2 gather_fusion.1
  15.1 2.4 collective-permute-done
  17.6 1.5 collective-permute-done.1
  19.2 1.6 collective-permute-start.2
  20.8 10.4 %all_gather.6 = f32[32,1,1024]{2,0,1:T(8,128)S(1)} all-gather(f32[32,1,128]{2,0,1:T(8,128)S(1)} %slice.669), channel_id=1, replica_groups=mesh['lon'=8,'lat'=4] {'lon'}, dimensions={2}, use_global_device_ids=true | all-gather | bytes 147456 | tf_op jit(solution)/shard_map/all_gather | solution.py:178
  31.4 0.7 gather_fusion.2
  32.1 2.3 collective-permute-start.3
  34.4 1.7 collective-permute-done.3
  36.5 0.5 copy-done.2
  37.3 0.3 fusion.128
  37.6 0.3 fusion.116
  38.1 0.8 fusion.230
  38.9 2.6 collective-permute-start.5
  41.6 11.3 %all_gather.7 = f32[32,1,1024]{0,2,1:T(8,128)S(1)} all-gather(f32[32,1,128]{0,2,1:T(8,128)S(1)} %copy.47), channel_id=1, replica_groups=mesh['lon'=8,'lat'=4] {'lon'}, dimensions={2}, use_global_device_ids=true | all-gather | bytes 147456 | tf_op jit(solution)/shard_map/all_gather | solution.py:178
  53.0 0.7 gather_fusion.3
  53.8 4.1 %collective-permute-start.7 = (f32[32,1,130]{2,0,1:T(8,128)S(1)}, f32[32,1,130]{2,0,1:T(8,128)S(1)}, u32[]{:S(2)}, u32[]{:S(2)}) collective-permute-start(f32[32,1,130]{2,0,1:T(8,128)S(1)} %get-tuple-element.17), channel_id=1, source_target_pairs={{1,0},{2,1},{3,2},{0,3},{5,4},{6,5},{7,6},{4,7},{9,8},{10,9},{11,1... | collective-permute-start | bytes 49928 | tf_op jit(solution)/shard_map/ppermute | solution.py:22
  57.9 5.7 %collective-permute-done.6 = f32[32,1,130]{2,0,1:T(8,128)S(1)} collective-permute-done((f32[32,1,130]{2,0,1:T(8,128)S(1)}, f32[32,1,130]{2,0,1:T(8,128)S(1)}, u32[]{:S(2)}, u32[]{:S(2)}) %collective-permute-start.6) | collective-permute-done | bytes 16672 | tf_op jit(solution)/shard_map/ppermute | solution.py:20
  65.0 2.6 collective-permute-start.9
  67.7 0.3 fusion.158
  68.0 0.7 copy.43
  68.7 2.9 %collective-permute-done.8 = bf16[40,16,1]{2,0,1:T(8,128)(2,1)S(1)} collective-permute-done((bf16[40,16,1]{2,0,1:T(8,128)(2,1)S(1)}, bf16[40,16,1]{2,0,1:T(8,128)(2,1)S(1)}, u32[]{:S(2)}, u32[]{:S(2)}) %collective-permute-start.8) | collective-permute-done | bytes 1312 | tf_op jit(solution)/shard_map/ppermute | solution.py:20
  71.8 2.0 collective-permute-start.10
  73.9 1.6 collective-permute-done.11
  75.5 1.9 collective-permute-done.10
  77.4 0.3 maximum_maximum_fusion.1
  77.7 0.3 fusion.66
  78.0 0.3 fusion.60
  78.3 0.3 fusion.71
  78.6 0.3 fusion.55
  78.9 0.3 convolution_add_fusion.11
  79.1 0.3 convolution_add_fusion.10
  79.4 0.3 fusion.4
  79.7 0.3 fusion.3
  80.0 0.3 convolution_add_fusion.7
  80.3 0.4 multiply_convert_fusion.1
  80.7 0.3 multiply_convert_fusion
  81.3 0.3 convolution_add_fusion.5
  81.6 0.3 convolution_add_fusion.4
  81.9 0.3 fusion.5
  82.2 0.3 fusion.6
  82.5 0.3 convolution_add_fusion.1
  82.8 0.4 fusion.9
  83.2 0.3 fusion.8
  85.2 2.6 collective-permute-start.13
  88.1 6.4 %collective-permute-done.12 = bf16[64,16,1]{2,0,1:T(8,128)(2,1)S(1)} collective-permute-done((bf16[64,16,1]{2,0,1:T(8,128)(2,1)S(1)}, bf16[64,16,1]{2,0,1:T(8,128)(2,1)S(1)}, u32[]{:S(2)}, u32[]{:S(2)}) %collective-permute-start.12) | collective-permute-done | bytes 2080 | tf_op jit(solution)/shard_map/ppermute | solution.py:20
  95.3 2.2 collective-permute-start.14
  97.5 1.1 collective-permute-done.15
  98.6 2.6 collective-permute-done.14
  101.2 0.5 maximum_maximum_fusion
  101.9 0.3 fusion.43
  102.2 0.3 fusion.31
  103.3 0.3 fusion.27
  104.4 0.7 pad_maximum_fusion.17
  105.3 0.3 convolution_add_fusion.16
  105.8 0.3 fusion.12
  106.6 0.7 copy.44
  107.3 115.0 %all-reduce.2.cloned.1.call-done = f32[27136]{0:T(1024)} async-done(((f32[27136]{0:T(1024)}), f32[27136]{0:T(1024)}) %all-reduce.2.cloned.1.call-update) | async-done | bytes 108560 | tf_op jit(solution)/shard_map/psum | solution.py:231
  222.3 37.5 %gather_fusion = f32[8192]{0:T(1024)S(1)} fusion(f32[27136]{0:T(1024)} %all-reduce.2.cloned.1.call-done, s32[8192]{0:T(1024)S(1)} %fusion.151), kind=kCustom, calls=%fused_computation.3 | custom fusion | bytes 98304 | tf_op jit(solution)/shard_map/jit(_take)/gather | solution.py:231
  259.8 0.6 and_select_fusion
  (107 shorter events, 9.5 us)
Async XLA Ops:
  7.2 73.5 %copy-start = (bf16[64,64]{1,0:T(8,128)(2,1)S(1)}, bf16[64,64]{1,0:T(8,128)(2,1)}, u32[]{:S(2)}) copy-start(bf16[64,64]{1,0:T(8,128)(2,1)} %param.18) | copy-start | bytes 24580
  7.2 215.1 %all-reduce.2.cloned.1.call-start = ((), (), s32[]{:S(2)}) async-start(), calls=%async_computation | async-start | bytes 221184 | tf_op jit(solution)/shard_map/psum | solution.py:231
  9.8 3.6 %copy-start.1 = (s32[1024]{0:T(1024)S(1)}, s32[1024]{0:T(1024)}, u32[]{:S(2)}) copy-start(s32[1024]{0:T(1024)} %param.16) | copy-start | bytes 12292
  10.0 4.7 %copy-start.6 = (bf16[16,16,128]{2,1,0:T(8,128)(2,1)S(1)}, bf16[16,16,128]{2,1,0:T(8,128)(2,1)}, u32[]{:S(2)}) copy-start(bf16[16,16,128]{2,1,0:T(8,128)(2,1)} %param.20) | copy-start | bytes 196612
  10.0 7.6 %collective-permute-start = (f32[32,16,1]{2,0,1:T(8,128)S(1)}, f32[32,16,1]{2,0,1:T(8,128)S(1)}, u32[]{:S(2)}, u32[]{:S(2)}) collective-permute-start(f32[32,16,1]{2,0,1:T(8,128)S(1)} %get-tuple-element.31), channel_id=1, source_target_pairs={{0,4},{4,8},{8,12},{12,16},{16,20},{20,24},{24,28},{28,0},{1,5},{5... | collective-permute-start | bytes 6152 | tf_op jit(solution)/shard_map/ppermute | solution.py:20
  10.5 8.6 %collective-permute-start.1 = (f32[32,16,1]{2,0,1:T(8,128)S(1)}, f32[32,16,1]{2,0,1:T(8,128)S(1)}, u32[]{:S(2)}, u32[]{:S(2)}) collective-permute-start(f32[32,16,1]{2,0,1:T(8,128)S(1)} %get-tuple-element.32), channel_id=1, source_target_pairs={{4,0},{8,4},{12,8},{16,12},{20,16},{24,20},{28,24},{0,28},{5,1},{9... | collective-permute-start | bytes 6152 | tf_op jit(solution)/shard_map/ppermute | solution.py:22
  13.5 1.3 copy-start.5
  13.5 1.3 copy-start.4
  19.2 15.2 %collective-permute-start.2 = (f32[32,1,130]{2,0,1:T(8,128)S(1)}, f32[32,1,130]{2,0,1:T(8,128)S(1)}, u32[]{:S(2)}, u32[]{:S(2)}) collective-permute-start(f32[32,1,130]{2,0,1:T(8,128)S(1)} %get-tuple-element.20), channel_id=1, source_target_pairs={{0,1},{1,2},{2,3},{3,0},{4,5},{5,6},{6,7},{7,4},{8,9},{9,10},{10,1... | collective-permute-start | bytes 49928 | tf_op jit(solution)/shard_map/ppermute | solution.py:20
  31.2 4.9 %copy-start.8 = (f32[32]{0:T(128)S(1)}, f32[32]{0:T(128)}, u32[]{:S(2)}) copy-start(f32[32]{0:T(128)} %constant.106.clone.1) | copy-start | bytes 388
  32.1 4.0 %collective-permute-start.3 = (f32[32,1,130]{2,0,1:T(8,128)S(1)}, f32[32,1,130]{2,0,1:T(8,128)S(1)}, u32[]{:S(2)}, u32[]{:S(2)}) collective-permute-start(f32[32,1,130]{2,0,1:T(8,128)S(1)} %get-tuple-element.19), channel_id=1, source_target_pairs={{1,0},{2,1},{3,2},{0,3},{5,4},{6,5},{7,6},{4,7},{9,8},{10,9},{11,1... | collective-permute-start | bytes 49928 | tf_op jit(solution)/shard_map/ppermute | solution.py:22
  36.2 0.8 copy-start.2
  36.2 0.8 copy-start.3
  38.9 14.8 %collective-permute-start.4 = (f32[32,16,1]{2,0,1:T(8,128)}, f32[32,16,1]{2,0,1:T(8,128)S(1)}, u32[]{:S(2)}, u32[]{:S(2)}) collective-permute-start(f32[32,16,1]{2,0,1:T(8,128)} %get-tuple-element.29), channel_id=1, source_target_pairs={{0,4},{4,8},{8,12},{12,16},{16,20},{20,24},{24,28},{28,0},{1,5},{5... | collective-permute-start | bytes 6152 | tf_op jit(solution)/shard_map/ppermute | solution.py:20
  38.9 14.8 %collective-permute-start.5 = (f32[32,16,1]{2,0,1:T(8,128)S(1)}, f32[32,16,1]{2,0,1:T(8,128)S(1)}, u32[]{:S(2)}, u32[]{:S(2)}) collective-permute-start(f32[32,16,1]{2,0,1:T(8,128)S(1)} %get-tuple-element.30), channel_id=1, source_target_pairs={{4,0},{8,4},{12,8},{16,12},{20,16},{24,20},{28,24},{0,28},{5,1},{9... | collective-permute-start | bytes 6152 | tf_op jit(solution)/shard_map/ppermute | solution.py:22
  53.8 9.8 %collective-permute-start.7 = (f32[32,1,130]{2,0,1:T(8,128)S(1)}, f32[32,1,130]{2,0,1:T(8,128)S(1)}, u32[]{:S(2)}, u32[]{:S(2)}) collective-permute-start(f32[32,1,130]{2,0,1:T(8,128)S(1)} %get-tuple-element.17), channel_id=1, source_target_pairs={{1,0},{2,1},{3,2},{0,3},{5,4},{6,5},{7,6},{4,7},{9,8},{10,9},{11,1... | collective-permute-start | bytes 49928 | tf_op jit(solution)/shard_map/ppermute | solution.py:22
  57.9 5.7 %collective-permute-start.6 = (f32[32,1,130]{2,0,1:T(8,128)S(1)}, f32[32,1,130]{2,0,1:T(8,128)S(1)}, u32[]{:S(2)}, u32[]{:S(2)}) collective-permute-start(f32[32,1,130]{2,0,1:T(8,128)S(1)} %get-tuple-element.18), channel_id=1, source_target_pairs={{0,1},{1,2},{2,3},{3,0},{4,5},{5,6},{6,7},{7,4},{8,9},{9,10},{10,1... | collective-permute-start | bytes 49928 | tf_op jit(solution)/shard_map/ppermute | solution.py:20
  64.7 2.9 %copy-start.7 = (bf16[9,64,24]{1,2,0:T(8,128)(2,1)S(1)}, bf16[9,64,24]{1,2,0:T(8,128)(2,1)}, u32[]{:S(2)}) copy-start(bf16[9,64,24]{1,2,0:T(8,128)(2,1)} %param.17) | copy-start | bytes 82948
  65.0 6.6 %collective-permute-start.8 = (bf16[40,16,1]{2,0,1:T(8,128)(2,1)S(1)}, bf16[40,16,1]{2,0,1:T(8,128)(2,1)S(1)}, u32[]{:S(2)}, u32[]{:S(2)}) collective-permute-start(bf16[40,16,1]{2,0,1:T(8,128)(2,1)S(1)} %get-tuple-element.35), channel_id=1, source_target_pairs={{0,4},{4,8},{8,12},{12,16},{16,20},{20,24},{24,28},{28,0},{1,5},{5... | collective-permute-start | bytes 3848 | tf_op jit(solution)/shard_map/ppermute | solution.py:20
  65.0 6.5 %collective-permute-start.9 = (bf16[40,16,1]{2,0,1:T(8,128)(2,1)S(1)}, bf16[40,16,1]{2,0,1:T(8,128)(2,1)S(1)}, u32[]{:S(2)}, u32[]{:S(2)}) collective-permute-start(bf16[40,16,1]{2,0,1:T(8,128)(2,1)S(1)} %get-tuple-element.36), channel_id=1, source_target_pairs={{4,0},{8,4},{12,8},{16,12},{20,16},{24,20},{28,24},{0,28},{5,1},{9... | collective-permute-start | bytes 3848 | tf_op jit(solution)/shard_map/ppermute | solution.py:22
  71.7 3.8 %collective-permute-start.11 = (bf16[40,1,130]{2,0,1:T(8,128)(2,1)S(1)}, bf16[40,1,130]{2,0,1:T(8,128)(2,1)S(1)}, u32[]{:S(2)}, u32[]{:S(2)}) collective-permute-start(bf16[40,1,130]{2,0,1:T(8,128)(2,1)S(1)} %get-tuple-element.24), channel_id=1, source_target_pairs={{1,0},{2,1},{3,2},{0,3},{5,4},{6,5},{7,6},{4,7},{9,8},{10,9},{11,1... | collective-permute-start | bytes 31208 | tf_op jit(solution)/shard_map/ppermute | solution.py:22
  71.8 5.6 %collective-permute-start.10 = (bf16[40,1,130]{2,0,1:T(8,128)(2,1)S(1)}, bf16[40,1,130]{2,0,1:T(8,128)(2,1)S(1)}, u32[]{:S(2)}, u32[]{:S(2)}) collective-permute-start(bf16[40,1,130]{2,0,1:T(8,128)(2,1)S(1)} %get-tuple-element.23), channel_id=1, source_target_pairs={{0,1},{1,2},{2,3},{3,0},{4,5},{5,6},{6,7},{7,4},{8,9},{9,10},{10,1... | collective-permute-start | bytes 31208 | tf_op jit(solution)/shard_map/ppermute | solution.py:20
  85.2 9.3 %collective-permute-start.12 = (bf16[64,16,1]{2,0,1:T(8,128)(2,1)S(1)}, bf16[64,16,1]{2,0,1:T(8,128)(2,1)S(1)}, u32[]{:S(2)}, u32[]{:S(2)}) collective-permute-start(bf16[64,16,1]{2,0,1:T(8,128)(2,1)S(1)} %get-tuple-element.25), channel_id=1, source_target_pairs={{0,4},{4,8},{8,12},{12,16},{16,20},{20,24},{24,28},{28,0},{1,5},{5... | collective-permute-start | bytes 6152 | tf_op jit(solution)/shard_map/ppermute | solution.py:20
  85.2 9.3 %collective-permute-start.13 = (bf16[64,16,1]{2,0,1:T(8,128)(2,1)S(1)}, bf16[64,16,1]{2,0,1:T(8,128)(2,1)S(1)}, u32[]{:S(2)}, u32[]{:S(2)}) collective-permute-start(bf16[64,16,1]{2,0,1:T(8,128)(2,1)S(1)} %get-tuple-element.26), channel_id=1, source_target_pairs={{4,0},{8,4},{12,8},{16,12},{20,16},{24,20},{28,24},{0,28},{5,1},{9... | collective-permute-start | bytes 6152 | tf_op jit(solution)/shard_map/ppermute | solution.py:22
  94.6 4.0 %collective-permute-start.15 = (bf16[64,1,130]{2,0,1:T(8,128)(2,1)S(1)}, bf16[64,1,130]{2,0,1:T(8,128)(2,1)S(1)}, u32[]{:S(2)}, u32[]{:S(2)}) collective-permute-start(bf16[64,1,130]{2,0,1:T(8,128)(2,1)S(1)} %get-tuple-element.16), channel_id=1, source_target_pairs={{1,0},{2,1},{3,2},{0,3},{5,4},{6,5},{7,6},{4,7},{9,8},{10,9},{11,1... | collective-permute-start | bytes 49928 | tf_op jit(solution)/shard_map/ppermute | solution.py:22
  95.3 5.9 %collective-permute-start.14 = (bf16[64,1,130]{2,0,1:T(8,128)(2,1)S(1)}, bf16[64,1,130]{2,0,1:T(8,128)(2,1)S(1)}, u32[]{:S(2)}, u32[]{:S(2)}) collective-permute-start(bf16[64,1,130]{2,0,1:T(8,128)(2,1)S(1)} %get-tuple-element.15), channel_id=1, source_target_pairs={{0,1},{1,2},{2,3},{3,0},{4,5},{5,6},{6,7},{7,4},{8,9},{9,10},{10,1... | collective-permute-start | bytes 49928 | tf_op jit(solution)/shard_map/ppermute | solution.py:20
Sparse Core Ops, SparseCore 0:
  105.2 117.0 all-reduce.1
where the time goes:
time: 268 us; the launch traced here: 267 us
  waiting for transfers between devices  143 us (53%)
  local copies, waits for them, and re-layouts  44.2 us (16%)
  starting transfers between devices  23.8 us (9%)
  blocking collectives  21.7 us (8%)
  between operations  14.6 us (5%)
  matrix products  12.3 us (5%)
  other arithmetic  7.77 us (3%)
    psum x1, waiting for transfers between devices, on_device(): grad_active = jnp.take(lax.psum(flat, ('lon', 'lat')), active_index)  115 us
    gather x1, local copies, waits for them, and re-layouts, on_device(): grad_active = jnp.take(lax.psum(flat, ('lon', 'lat')), active_index)  37.5 us
    ppermute x8, waiting for transfers between devices, padded_2(): lax.ppermute(tail, axis, [(i, (i + 1) % count) for i in range(count)])  21.9 us
    all_gather x2, blocking collectives, on_device(): lax.all_gather(source[:, row_count - 1:, :], 'lon', axis=2, tiled=True)  21.7 us
    ppermute x8, starting transfers between devices, padded_2(): lax.ppermute(head, axis, [((i + 1) % count, i) for i in range(count)])  17.4 us
    ppermute x8, starting transfers between devices, padded_2(): lax.ppermute(tail, axis, [(i, (i + 1) % count) for i in range(count)])  6.35 us
    ppermute x8, waiting for transfers between devices, padded_2(): lax.ppermute(head, axis, [((i + 1) % count, i) for i in range(count)])  5.87 us
  transfers between devices with their start and end apart: 17, of which 11 were waited for; matrix products, arithmetic and copies ran while one was open for 3% of the time, Pallas kernels for 0%

commit v1 on v0

v1 whole, which is shorter than its diff:
```python
import functools
import math

import jax
import jax.numpy as jnp
from jax import lax
from jax.experimental import pallas as pl
from jax.experimental.pallas import tpu as pltpu
from jax.sharding import PartitionSpec as P

MESH = pl.DeviceIdType.MESH
F32 = jnp.float32
BF16 = jnp.bfloat16
WIDE = 4
VMEM = pl.BlockSpec(memory_space=pltpu.VMEM)
SMEM = pl.BlockSpec(memory_space=pltpu.SMEM)


def masked_row(ocean, kappa, depth, cot, row, scale):
    levels = lax.broadcasted_iota(jnp.int32, (8, 128), 0)
    wet = (levels < depth[pl.ds(row, 1), :]).astype(F32)
    u = ocean[0, :, row, :] * wet
    v = ocean[1, :, row, :] * wet
    t = ocean[2, :, row, :] * wet
    k = kappa[:, row, :] * wet
    wet2 = jnp.concatenate([wet, wet], axis=0)
    g = scale * wet2 * cot[row].astype(F32)
    return u, v, t, k, g, wet2


def exchange_kernel(
    n_lon, n_lat, scale, ocean, kappa, depth, cot, north, south, sides, tops,
    rows, packed, top_own, row_send, row_recv, side_send, side_recv, top_send, top_recv,
):
    lon = lax.axis_index("lon")
    lat = lax.axis_index("lat")
    count = rows.shape[0]
    east = lax.rem(lon + 1, n_lon)
    west = lax.rem(lon + n_lon - 1, n_lon)
    has_north = lat < n_lat - 1
    has_south = lat > 0
    at_top = lat == n_lat - 1

    barrier = pltpu.get_barrier_semaphore()

    def greet(to_lat, to_lon):
        pl.semaphore_signal(barrier, inc=1, device_id=(to_lon, to_lat), device_id_type=MESH)

    for step in range(1, n_lon):
        greet(lat, lax.rem(lon + step, n_lon))

    @pl.when(has_north)
    def _():
        for to in (lon, east, west):
            greet(lat + 1, to)

    @pl.when(has_south)
    def _():
        for to in (lon, east, west):
            greet(lat - 1, to)

    lanes = lax.broadcasted_iota(jnp.int32, (48, 128), 1)
    acc = jnp.zeros((48, 128), F32)
    for row in range(count):
        u, v, t, k, g, _ = masked_row(ocean, kappa, depth, cot, row, scale)
        line = jnp.concatenate([u, v, t, k, g], axis=0)
        rows[row] = line.astype(BF16)
        acc = jnp.where(lanes // 8 == row, pltpu.roll(line, (4 + 8 * row) % 128, axis=1), acc)
    packed[...] = acc.astype(BF16)

    sides_open = has_north.astype(jnp.int32) + has_south.astype(jnp.int32)
    pl.semaphore_wait(barrier, n_lon - 1 + 3 * sides_open)

    def send_rows(start, dst, slot, to_lat):
        return pltpu.make_async_remote_copy(
            src_ref=rows.at[pl.ds(start, WIDE)], dst_ref=dst, send_sem=row_send.at[slot],
            recv_sem=row_recv.at[slot], device_id=(lon, to_lat), device_id_type=MESH,
        )

    def send_side(slot, to_lat, to_lon):
        return pltpu.make_async_remote_copy(
            src_ref=packed, dst_ref=sides.at[slot], send_sem=side_send.at[slot],
            recv_sem=side_recv.at[slot], device_id=(to_lon, to_lat), device_id_type=MESH,
        )

    def send_top(step):
        return pltpu.make_async_remote_copy(
            src_ref=rows.at[pl.ds(count - 2, 2)], dst_ref=tops.at[lon], send_sem=top_send.at[step],
            recv_sem=top_recv.at[lon], device_id=(lax.rem(lon + step, n_lon), lat), device_id_type=MESH,
        )

    def top_from(step):
        peer = lax.rem(lon + step, n_lon)
        return pltpu.make_async_remote_copy(
            src_ref=rows.at[pl.ds(count - 2, 2)], dst_ref=tops.at[peer], send_sem=top_send.at[step],
            recv_sem=top_recv.at[peer], device_id=(peer, lat), device_id_type=MESH,
        )

    to_north = send_rows(count - WIDE, south, 0, lat + 1)
    to_south = send_rows(0, north, 1, lat - 1)
    same = [send_side(0, lat, east), send_side(1, lat, west)]
    up = [send_side(2, lat + 1, east), send_side(3, lat + 1, west)]
    down = [send_side(4, lat - 1, east), send_side(5, lat - 1, west)]

    @pl.when(has_north)
    def _():
        to_north.start()

    @pl.when(has_south)
    def _():
        to_south.start()

    @pl.when(at_top)
    def _():
        for step in range(1, n_lon):
            send_top(step).start()

    for copy in same:
        copy.start()

    @pl.when(has_north)
    def _():
        for copy in up:
            copy.start()

    @pl.when(has_south)
    def _():
        for copy in down:
            copy.start()

    for copy in same:
        copy.wait()

    @pl.when(has_north)
    def _():
        to_north.wait_send()
        to_south.wait_recv()
        for copy in up:
            copy.wait_send()
        for copy in down:
            copy.wait_recv()

    @pl.when(has_south)
    def _():
        to_south.wait_send()
        to_north.wait_recv()
        for copy in down:
            copy.wait_send()
        for copy in up:
            copy.wait_recv()

    @pl.when(at_top)
    def _():
        tops[lon] = rows[count - 2 : count]
        for step in range(1, n_lon):
            send_top(step).wait_send()
            top_from(step).wait_recv()


def dot(a, b):
    return jnp.dot(a, b, preferred_element_type=F32)


def dot_cells(a, b):
    return lax.dot_general(a, b, (((1,), (1,)), ((), ())), preferred_element_type=F32)


def slope(pre, sigma):
    return sigma * (1.0 + pre * (1.0 - sigma))


def sigmoid(pre):
    return 1.0 / (1.0 + jnp.exp(-pre))


def east_of(own, rim, lane):
    a = pltpu.roll(own, 127, axis=own.ndim - 1)
    b = pltpu.roll(rim, 127, axis=own.ndim - 1)
    return jnp.where(lane == 127, b, a), jnp.where(lane == 127, a, b)


def west_of(own, rim, lane):
    a = pltpu.roll(own, 1, axis=own.ndim - 1)
    b = pltpu.roll(rim, 1, axis=own.ndim - 1)
    return jnp.where(lane == 0, b, a), jnp.where(lane == 0, a, b)


def compute_kernel(
    n_lon, n_lat, scale, fold, ocean, kappa, depth, cot, north, south, sides, tops,
    w_first, w_mix, w_mix_t, w_last, w_back, krow, klane, coriolis,
    state, closure, picked,
    f_a, f_b, h_a, h_b, ks_a, ks_b, g_own, wet2s, patches, slope1, slope2, hid1, hid2, hshift, gpatch, dmix, dfirst, table,
):
    lon = lax.axis_index("lon")
    lat = lax.axis_index("lat")
    count = ocean.shape[2]
    total = count + 2 * WIDE
    at_top = lat == n_lat - 1
    at_bottom = lat == 0
    lane = lax.broadcasted_iota(jnp.int32, (8, 128), 1)
    level = lax.broadcasted_iota(jnp.int32, (8, 128), 0)
    lane48 = lax.broadcasted_iota(jnp.int32, (48, 128), 1)
    zero48 = jnp.zeros((48, 128), F32)

    def merge(low):
        odd = lane48 % 8 >= 4
        return jnp.where(odd, sides[low + 1].astype(F32), sides[low].astype(F32))

    def put(row, own, rim):
        for f in range(4):
            if own is not None:
                f_a[row, f] = own[8 * f : 8 * f + 8]
            f_b[row, f] = rim[8 * f : 8 * f + 8]
        if WIDE - 1 <= row <= WIDE + count:
            if own is not None:
                g_own[row - WIDE + 1, 0] = own[32:48]
            g_own[row - WIDE + 1, 1] = rim[32:48]

    def unpack(side, row):
        return pltpu.roll(side, (128 - 4 - 8 * row) % 128, axis=1)

    mid = merge(0)
    below = jnp.where(at_bottom, zero48, merge(2))
    above = jnp.where(at_top, zero48, merge(4))
    for row in range(count):
        u, v, t, k, g, wet2 = masked_row(ocean, kappa, depth, cot, row, scale)
        own = jnp.concatenate([u, v, t, k, g.astype(BF16).astype(F32)], axis=0)
        put(row + WIDE, own, unpack(mid, row))
        wet2s[row] = wet2
    for row in range(WIDE):
        put(row, jnp.where(at_bottom, zero48, south[row].astype(F32)), unpack(below, count - WIDE + row))
        put(WIDE + count + row, jnp.where(at_top, zero48, north[row].astype(F32)), unpack(above, row))

    @pl.when(at_top)
    def _():
        nx = n_lon * 128
        s = fold[0]
        at = lax.broadcasted_iota(jnp.int32, (128, 256), 0)
        pos = lax.broadcasted_iota(jnp.int32, (1, 256), 1)
        col = lon * 128 + jnp.where(pos >= 192, pos - 256, pos)
        col = jnp.where(col < 0, col + nx, col)
        col = jnp.where(col >= nx, col - nx, col)
        partner = s - col
        partner = jnp.where(partner < 0, partner + nx, partner)
        res = jnp.zeros((64, 256), F32)
        for j in range(n_lon):
            pick = jnp.where(at + 128 * j == partner, 1.0, 0.0).astype(BF16)
            both = jnp.concatenate([tops[j, 1, 0:32], tops[j, 0, 0:32]], axis=0)
            res = res + dot(both, pick)
        for q in range(2):
            for f in range(4):
                sign = -1.0 if f < 2 else 1.0
                part = sign * res[32 * q + 8 * f : 32 * q + 8 * f + 8]
                f_a[WIDE + count + q, f] = part[:, :128]
                f_b[WIDE + count + q, f] = part[:, 128:]

    def roots(r, _):
        k_a, k_b = f_a[r, 3], f_b[r, 3]
        e_a, e_b = east_of(k_a, k_b, lane)
        ks_a[r, 0] = jnp.sqrt(k_a * e_a)
        ks_b[r, 0] = jnp.sqrt(k_b * e_b)
        ks_a[r, 1] = jnp.sqrt(k_a * f_a[r + 1, 3])
        ks_b[r, 1] = jnp.sqrt(k_b * f_b[r + 1, 3])
        return 0

    lax.fori_loop(0, total - 1, roots, 0, unroll=2)

    def summed(x):
        for d in (1, 2, 4):
            x = x + jnp.where(level >= d, pltpu.roll(x, d, axis=0), 0.0)
        return x

    def step(src_a, src_b, dst_a, dst_b):
        def body(r, _):
            fr = coriolis[r]
            ke_a, ke_b = ks_a[r, 0], ks_b[r, 0]
            kw_a, kw_b = west_of(ke_a, ke_b, lane)
            coef = ((ke_a, kw_a, ks_a[r, 1], ks_a[r - 1, 1]), (ke_b, kw_b, ks_b[r, 1], ks_b[r - 1, 1]))
            mids, es, ws = [], [], []
            for f in range(3):
                a, b = src_a[r, f], src_b[r, f]
                mids.append((a, b))
                es.append(east_of(a, b, lane))
                ws.append(west_of(a, b, lane))
            for i, (src, dst, k_own) in enumerate(((src_a, dst_a, f_a[r, 3]), (src_b, dst_b, f_b[r, 3]))):
                wet = jnp.where(k_own > 0, 1.0, 0.0)
                ke, kw, kn, ks = coef[i]
                u, v, t = mids[0][i], mids[1][i], mids[2][i]
                ns = [src[r + 1, f] for f in range(3)]
                ss = [src[r - 1, f] for f in range(3)]
                outs = []
                for f in range(3):
                    m = mids[f][i]
                    outs.append(
                        m + ke * (es[f][i] - m) + kw * (ws[f][i] - m) + kn * (ns[f] - m) + ks * (ss[f] - m)
                    )
                dx = es[2][i] - ws[2][i]
                dy = ns[2] - ss[2]
                dst[r, 0] = wet * (outs[0] + fr * v - 0.025 * summed(dx))
                dst[r, 1] = wet * (outs[1] - fr * u - 0.025 * summed(dy))
                dst[r, 2] = wet * (outs[2] - 0.125 * (u * dx + v * dy))
            return 0

        return body

    lax.fori_loop(1, total - 1, step(f_a, f_b, h_a, h_b), 0, unroll=2)
    lax.fori_loop(2, total - 2, step(h_a, h_b, f_a, f_b), 0, unroll=2)
    for row in range(count):
        for f in range(3):
            state[f, :, row, :] = f_a[row + WIDE, f]

    lane24 = lax.broadcasted_iota(jnp.int32, (24, 128), 1)
    lane72 = lax.broadcasted_iota(jnp.int32, (72, 128), 1)
    pad8 = jnp.zeros((8, 128), F32)
    lines = []
    side = jnp.zeros((72, 128), F32)
    for q in range(count + 4):
        a = jnp.concatenate([f_a[q + 2, f] for f in range(3)], axis=0)
        b = jnp.concatenate([f_b[q + 2, f] for f in range(3)], axis=0)
        if q < 2:
            a, b = jnp.where(at_bottom, 0.0, a), jnp.where(at_bottom, 0.0, b)
        if q >= count + 2:
            a, b = jnp.where(at_top, 0.0, a), jnp.where(at_top, 0.0, b)
        e_a, e_b = east_of(a, b, lane24)
        w_a, w_b = west_of(a, b, lane24)
        lines.append(jnp.concatenate([w_a, a, e_a], axis=0))
        rim = jnp.concatenate([w_b, b, e_b], axis=0)
        side = jnp.where(lane72 // 2 == q, pltpu.roll(rim, (1 + 2 * q) % 128, axis=1), side)
        if q >= 2:
            r = q - 2
            patches[:, 128 * r : 128 * r + 128] = jnp.concatenate(lines[-3:] + [pad8], axis=0).astype(BF16)
    span = (count + 2) * 128
    patches[:, span : span + 128] = jnp.concatenate(
        [side, pltpu.roll(side, 126, axis=1), pltpu.roll(side, 124, axis=1), pad8], axis=0
    ).astype(BF16)
    patches[:, span + 128 :] = jnp.zeros((224, patches.shape[1] - span - 128), BF16)

    for start in range(0, patches.shape[1], 256):
        pre1 = dot(w_first[...], patches[:, start : start + 256])
        s1 = sigmoid(pre1)
        h1 = (pre1 * s1).astype(BF16)
        pre2 = dot(w_mix[...], h1)
        s2 = sigmoid(pre2)
        hid1[:, start : start + 256] = h1
        hid2[:, start : start + 256] = (pre2 * s2).astype(BF16).astype(F32)
        slope1[:, start : start + 256] = slope(pre1, s1)
        slope2[:, start : start + 256] = slope(pre2, s2)

    lane64 = lax.broadcasted_iota(jnp.int32, (64, 128), 1)
    lane16 = lax.broadcasted_iota(jnp.int32, (16, 128), 1)
    edge = hid2[:, span : span + 128]
    for r in range(count + 2):
        own = hid2[:, 128 * r : 128 * r + 128]
        to_w = jnp.where(lane64 == 0, pltpu.roll(edge, (128 - 2 * r) % 128, axis=1), pltpu.roll(own, 1, axis=1))
        to_e = jnp.where(lane64 == 127, pltpu.roll(edge, 126 - 2 * r, axis=1), pltpu.roll(own, 127, axis=1))
        both = jnp.concatenate([to_w, own, to_e], axis=0)
        if r == 0:
            both = jnp.where(at_bottom, 0.0, both)
        if r == count + 1:
            both = jnp.where(at_top, 0.0, both)
        hshift[:, 128 * r : 128 * r + 128] = both.astype(BF16)
    glines = []
    for r in range(count + 2):
        a, b = g_own[r, 0], g_own[r, 1]
        e_a, _ = east_of(a, b, lane16)
        w_a, _ = west_of(a, b, lane16)
        glines.append(jnp.concatenate([e_a, a, w_a], axis=0))
        if r >= 2:
            j = r - 2
            gpatch[:, 128 * j : 128 * j + 128] = jnp.concatenate(glines[-3:][::-1], axis=0).astype(BF16)

    cells = count * 128
    for start in range(0, cells, 256):
        here = slice(start, start + 256)
        near = slice(start + 128, start + 384)
        out = dot(w_last[0], hshift[:, start : start + 256])
        out += dot(w_last[1], hshift[:, start + 128 : start + 384])
        out += dot(w_last[2], hshift[:, start + 256 : start + 512])
        for j in range(2):
            r = start // 128 + j
            closure[r] = (wet2s[r] * out[:, 128 * j : 128 * j + 128]).astype(BF16)
        back = dot(w_back[...], gpatch[:, here])
        dm = (back * slope2[:, near]).astype(BF16)
        dmix[:, here] = dm
        dfirst[:, here] = (dot(w_mix_t[...], dm) * slope1[:, near]).astype(BF16)

    g_first = dot_cells(dfirst[...], patches[:, 128 : 128 + cells])
    g_mix = dot_cells(dmix[...], hid1[:, 128 : 128 + cells])
    g_mid = gpatch[64:80, :]
    g_last = jnp.concatenate([dot_cells(g_mid, hshift[:, 128 * i : 128 * i + cells]) for i in range(3)], axis=1)
    table[0:64, :] = g_first[:, :128]
    table[64:128, 0:96] = g_first[:, 128:224]
    table[64:128, 96:128] = jnp.zeros((64, 32), F32)
    table[128:192, 64:128] = jnp.zeros((64, 64), F32)
    table[128:192, 0:64] = g_mix
    table[128:144, 64:128] = g_last[:, 512:576]
    for i in range(4):
        table[192 + 16 * i : 208 + 16 * i, :] = g_last[:, 128 * i : 128 * i + 128]
    q = table[...].T
    hi = q.astype(BF16)
    lo = (q - hi.astype(F32)).astype(BF16)
    split = jnp.concatenate([hi, lo], axis=0)
    at_row = lax.broadcasted_iota(jnp.int32, (256, 128), 0)
    at_lane = lax.broadcasted_iota(jnp.int32, (128, 128), 0)
    for j in range(0, krow.shape[0], 2):
        pick = jnp.concatenate(
            [jnp.where(at_row == krow[j + i : j + i + 1, :], 1.0, 0.0).astype(BF16) for i in range(2)], axis=1
        )
        got = dot(split, pick)
        got = got[:128] + got[128:]
        for i in range(2):
            mine = jnp.where(at_lane == klane[j + i : j + i + 1, :], got[:, 128 * i : 128 * i + 128], 0.0)
            picked[j + i : j + i + 1, :] = jnp.sum(mine, axis=0, keepdims=True)


def reduce_kernel(n_lon, n_lat, part, out, got_lon, got_lat, chunk, s1, r1, s2, r2, s3, r3):
    lon = lax.axis_index("lon")
    lat = lax.axis_index("lat")
    barrier = pltpu.get_barrier_semaphore()
    lons = [lax.rem(lon + step, n_lon) for step in range(1, n_lon)]
    lats = [lax.rem(lat + step, n_lat) for step in range(1, n_lat)]
    for to in lons:
        pl.semaphore_signal(barrier, inc=1, device_id=(to, lat), device_id_type=MESH)
    for to in lats:
        pl.semaphore_signal(barrier, inc=1, device_id=(lon, to), device_id_type=MESH)
    pl.semaphore_wait(barrier, n_lon + n_lat - 2)

    def copy(src, dst, ssem, rsem, to):
        return pltpu.make_async_remote_copy(
            src_ref=src, dst_ref=dst, send_sem=ssem, recv_sem=rsem, device_id=to, device_id_type=MESH
        )

    first = [copy(part.at[to], got_lon.at[lon], s1.at[to], r1.at[lon], (to, lat)) for to in lons]
    for c in first:
        c.start()
    got_lon[lon] = part[lon]
    for c, to in zip(first, lons):
        c.wait_send()
        copy(part.at[to], got_lon.at[to], s1.at[to], r1.at[to], (to, lat)).wait_recv()
    got_lat[lat] = jnp.sum(got_lon[...], axis=0)
    second = [copy(got_lat.at[lat], got_lat.at[lat], s2.at[to], r2.at[lat], (lon, to)) for to in lats]
    for c in second:
        c.start()
    for c, to in zip(second, lats):
        c.wait_send()
        copy(got_lat.at[to], got_lat.at[to], s2.at[to], r2.at[to], (lon, to)).wait_recv()
    chunk[...] = jnp.sum(got_lat[...], axis=0)
    third = [copy(chunk, out.at[lon], s3.at[to], r3.at[lon], (to, lat)) for to in lons]
    for c in third:
        c.start()
    out[lon] = chunk[...]
    for c, to in zip(third, lons):
        c.wait_send()
        copy(chunk, out.at[to], s3.at[to], r3.at[to], (to, lat)).wait_recv()


def entry_place(index):
    k, rest = index // 1536, index % 1536
    col = (k * 24) + rest % 24
    row_f, lane_f = rest // 24 + 64 * (col // 128), col % 128
    m = index - 13824
    row_m, lane_m = 128 + m // 64, m % 64
    m = index - 17920
    o, col = (m % 1024) // 64, (m // 1024) * 64 + m % 64
    spill = col >= 512
    row_l = jnp.where(spill, 128 + o, 192 + 16 * (col // 128) + o)
    lane_l = jnp.where(spill, 64 + col - 512, col % 128)
    row = jnp.where(index < 13824, row_f, jnp.where(index < 17920, row_m, row_l))
    lane = jnp.where(index < 13824, lane_f, jnp.where(index < 17920, lane_m, lane_l))
    return row, lane


def on_device(
    n_lon, n_lat, ocean_state, diffusivity, depth_levels, fold_pair, first_weight, mix_weight, last_weight,
    cotangent, active_index,
):
    count = ocean_state.shape[2]
    row_total = count * n_lat
    scale = 1.0 / math.sqrt(row_total * 128 * n_lon)
    cot = jnp.transpose(cotangent, (1, 0, 2))
    sds = jax.ShapeDtypeStruct
    dma = pltpu.SemaphoreType.DMA
    north, south, sides, tops = pl.pallas_call(
        functools.partial(exchange_kernel, n_lon, n_lat, scale),
        out_shape=[
            sds((WIDE, 48, 128), BF16), sds((WIDE, 48, 128), BF16), sds((6, 48, 128), BF16),
            sds((n_lon, 2, 48, 128), BF16),
        ],
        in_specs=[VMEM] * 4,
        out_specs=[VMEM] * 4,
        scratch_shapes=[
            pltpu.VMEM((count, 48, 128), BF16), pltpu.VMEM((48, 128), BF16), pltpu.VMEM((2, 48, 128), BF16),
            dma((2,)), dma((2,)), dma((6,)), dma((6,)), dma((n_lon,)), dma((n_lon,)),
        ],
        compiler_params=pltpu.CompilerParams(collective_id=0, has_side_effects=True),
        name="exchange",
    )(ocean_state, diffusivity, depth_levels, cot)

    row_ids = lax.axis_index("lat") * count - WIDE + jnp.arange(count + 2 * WIDE, dtype=jnp.int32)
    mirrored = jnp.where(row_ids >= row_total, 2 * row_total - 1 - row_ids, row_ids)
    rows_f = 0.25 * jnp.sin(math.pi * (mirrored.astype(F32) + 0.5) / row_total - 0.5 * math.pi)
    w_first = jnp.pad(jnp.transpose(first_weight, (1, 0, 2)).reshape(64, 216), ((0, 0), (0, 8)))
    w_last = jnp.transpose(last_weight.reshape(3, 3, 16, 64), (0, 2, 1, 3)).reshape(3, 16, 192)
    w_back = jnp.transpose(last_weight, (2, 0, 1)).reshape(64, 144)
    krow, klane = entry_place(active_index)
    picks = active_index.shape[0] // 128
    total = count + 2 * WIDE
    wide = (count + 4) * 128
    cells = count * 128
    state, closure, picked = pl.pallas_call(
        functools.partial(compute_kernel, n_lon, n_lat, scale),
        out_shape=[
            sds((3, 8, count, 128), F32), sds((count, 16, 128), BF16), sds((picks, 128), F32),
        ],
        in_specs=[SMEM] + [VMEM] * 15 + [SMEM],
        out_specs=[VMEM] * 3,
        scratch_shapes=[
            pltpu.VMEM((total, 4, 8, 128), F32), pltpu.VMEM((total, 4, 8, 128), F32),
            pltpu.VMEM((total, 3, 8, 128), F32), pltpu.VMEM((total, 3, 8, 128), F32),
            pltpu.VMEM((total, 2, 8, 128), F32), pltpu.VMEM((total, 2, 8, 128), F32),
            pltpu.VMEM((count + 2, 2, 16, 128), F32), pltpu.VMEM((count, 16, 128), F32),
            pltpu.VMEM((224, wide), BF16), pltpu.VMEM((64, wide), F32), pltpu.VMEM((64, wide), F32),
            pltpu.VMEM((64, wide), BF16), pltpu.VMEM((64, wide), F32), pltpu.VMEM((192, (count + 2) * 128), BF16),
            pltpu.VMEM((144, cells), BF16), pltpu.VMEM((64, cells), BF16), pltpu.VMEM((64, cells), BF16),
            pltpu.VMEM((256, 128), F32),
        ],
        compiler_params=pltpu.CompilerParams(vmem_limit_bytes=48 * 1024 * 1024),
        name="compute",
    )(
        fold_pair[:8], ocean_state, diffusivity, depth_levels, cot, north, south, sides, tops, w_first, mix_weight,
        mix_weight.T, w_last, w_back, krow.reshape(picks, 128), klane.reshape(picks, 128), rows_f,
    )

    depth = picks // n_lon
    reduced = pl.pallas_call(
        functools.partial(reduce_kernel, n_lon, n_lat),
        out_shape=sds((n_lon, depth, 128), F32),
        in_specs=[VMEM],
        out_specs=VMEM,
        scratch_shapes=[
            pltpu.VMEM((n_lon, depth, 128), F32), pltpu.VMEM((n_lat, depth, 128), F32), pltpu.VMEM((depth, 128), F32),
            dma((n_lon,)), dma((n_lon,)), dma((n_lat,)), dma((n_lat,)), dma((n_lon,)), dma((n_lon,)),
        ],
        compiler_params=pltpu.CompilerParams(collective_id=1, has_side_effects=True),
        name="reduce",
    )(picked.reshape(n_lon, depth, 128))
    return state, jnp.transpose(closure, (1, 0, 2)), reduced.reshape(-1)


def solution(mesh):
    in_specs = (
        P(None, None, "lat", "lon"), P(None, "lat", "lon"), P("lat", "lon"), P(), P(), P(), P(),
        P(None, "lat", "lon"), P(),
    )
    out_specs = (P(None, None, "lat", "lon"), P(None, "lat", "lon"), P())
    return jax.shard_map(
        functools.partial(on_device, mesh.shape["lon"], mesh.shape["lat"]),
        mesh=mesh, in_specs=in_specs, out_specs=out_specs, check_vma=False,
    )
```

time: 268 us -> 48.6 us (0.18)
  waiting for transfers between devices: 143 us -> 0 us
  Pallas kernels: 0 us -> 36.6 us
  local copies, waits for them, and re-layouts: 44.2 us -> 10.2 us
  starting transfers between devices: 23.8 us -> 0 us
  blocking collectives: 21.7 us -> 0 us
  between operations: 14.6 us -> 0.79 us
  matrix products: 12.3 us -> 0 us
  other arithmetic: 7.77 us -> 0.28 us
    psum x1 -> x0, waiting for transfers between devices: 115 us -> none  [on_device(): grad_active = jnp.take(lax.psum(flat, ('lon', 'lat')), active_index)]
    gather x6 -> x0, local copies, waits for them, and re-layouts: 40.1 us -> none  [the longest x1 37.5 us: on_device(): grad_active = jnp.take(lax.psum(flat, ('lon', 'lat')), active_index)]
    pallas_call x0 -> x3, Pallas kernels: none -> 36.6 us  [the longest x1 15.1 us: on_device(): pl.pallas_call(functools.partial(reduce_kernel, n_lon, n_lat), out_shape=...]
    ppermute x16 -> x0, waiting for transfers between devices: 27.8 us -> none  [the longest x8 21.9 us: padded_2(): lax.ppermute(tail, axis, [(i, (i + 1) % count) for i in range(count)])]
    ppermute x16 -> x0, starting transfers between devices: 23.8 us -> none  [the longest x8 17.4 us: padded_2(): lax.ppermute(head, axis, [((i + 1) % count, i) for i in range(count)])]
    all_gather x2 -> x0, blocking collectives: 21.7 us -> none  [on_device(): lax.all_gather(source[:, row_count - 1:, :], 'lon', axis=2, tiled=True)]
    dot_general x48 -> x0, matrix products: 12.3 us -> none  [the longest x18 4.71 us: convolve(): jnp.einsum('oc,cyx->oyx', weight[tap_index], padded[:, tap_row:tap_row +...]
    unnamed x22 -> x30, local copies, waits for them, and re-layouts: 2.15 us -> 8.36 us
  transfers between devices with their start and end apart: 17 -> 0, of which waited for: 11 -> 0; matrix products, arithmetic and copies ran while one was open for 3% -> 0% of each run, Pallas kernels for 0% -> 0%
where the time goes in v1:
time: 48.6 us; the launch traced here: 47.9 us
  Pallas kernels  36.6 us (75%)
  local copies, waits for them, and re-layouts  10.2 us (21%)
  between operations  0.79 us (2%)
    pallas_call x1, Pallas kernels, on_device(): pl.pallas_call(functools.partial(reduce_kernel, n_lon, n_lat), out_shape=...  15.1 us
    pallas_call x1, Pallas kernels, on_device(): pl.pallas_call(functools.partial(compute_kernel, n_lon, n_lat, scale), ou...  11.1 us
    pallas_call x1, Pallas kernels, on_device(): pl.pallas_call(functools.partial(exchange_kernel, n_lon, n_lat, scale), o...  10.4 us
    unnamed x30, local copies, waits for them, and re-layouts  8.36 us

profile of v1, /device:TPU:0, one launch (start us, length us, event | category | flops | bytes accessed | tf_op | source)
XLA Modules:
  0.0 47.9 jit_solution(1487255176738402500)
XLA Ops:
  0.6 0.0 copy-start.5
  0.7 0.7 %slice.3.fold = s32[8]{0:T(128)S(1)} slice(s32[1024]{0:T(1024)} %param.12), slice={[0:8]} | slice | bytes 64 | tf_op jit(solution)/shard_map/slice | solution.py:530
  1.4 0.0 copy-done.5
  1.4 0.1 copy.20
  1.5 0.9 %copy.19 = bf16[64,216]{1,0:T(8,128)(2,1)S(1)} copy(bf16[64,216]{0,1:T(8,128)(2,1)} %bitcast.30) | data formatting | bytes 55296 | tf_op jit(solution)/shard_map/reshape | solution.py:502
  2.4 0.0 copy-start.10
  2.4 0.7 %copy-done.10 = bf16[9,16,64]{2,1,0:T(8,128)(2,1)S(1)} copy-done((bf16[9,16,64]{2,1,0:T(8,128)(2,1)S(1)}, bf16[9,16,64]{2,1,0:T(8,128)(2,1)}, u32[]{:S(2)}) %copy-start.10) | copy-done | bytes 18456
  3.2 0.1 copy.22.w_back
  3.3 0.0 copy-start.11
  3.3 0.1 reshape.32.w_last
  3.4 0.7 %copy-done.11 = bf16[16,16,128]{2,1,0:T(8,128)(2,1)S(1)} copy-done((bf16[16,16,128]{2,1,0:T(8,128)(2,1)S(1)}, bf16[16,16,128]{2,1,0:T(8,128)(2,1)}, u32[]{:S(2)}) %copy-start.11) | copy-done | bytes 65560
  4.1 0.0 copy-start.12
  4.1 0.6 %copy.26 = bf16[16,16,128]{2,0,1:T(8,128)(2,1)} copy(bf16[16,16,128]{2,1,0:T(8,128)(2,1)S(1)} %copy-done.11) | data formatting | bytes 131072 | tf_op args[7]
  4.7 0.1 copy-done.12
  4.9 0.2 fusion.16
  5.1 0.0 copy-start
  5.1 0.0 copy-start.1
  5.1 0.0 copy-start.2
  5.1 0.0 copy-start.8
  5.1 10.4 %exchange.1 = (bf16[4,48,128]{2,1,0:T(8,128)(2,1)}, bf16[4,48,128]{2,1,0:T(8,128)(2,1)}, bf16[6,48,128]{2,1,0:T(8,128)(2,1)}, bf16[8,2,48,128]{3,2,1,0:T(8,128)(2,1)}) custom-call(f32[3,8,16,128]{3,2,1,0:T(8,128)} %ocean.3, f32[8,16,128]{2,1,0:T(8,128)} %kappa.3, s32[16,128]{1,0:T(8,128)} %depth.3, bf16[16,16,128]{2,1,0:T(8,128)(2,1)} %bitcast.21), custom_call_target="tpu_custom_call" | custom-call | tf_op jit(solution)/shard_map/exchange/pallas_call | solution.py:483
  15.6 0.0 copy-done
  15.6 0.0 copy-done.1
  15.6 0.0 copy-done.2
  15.6 0.0 copy-done.8
  15.6 0.0 copy-start.3
  15.6 0.9 %copy-done.3 = bf16[8,2,48,128]{3,2,1,0:T(8,128)(2,1)S(1)} copy-done((bf16[8,2,48,128]{3,2,1,0:T(8,128)(2,1)S(1)}, bf16[8,2,48,128]{3,2,1,0:T(8,128)(2,1)}, u32[]{:S(2)}) %copy-start.3) | copy-done | bytes 196632
  16.6 0.0 copy-start.4
  16.6 0.9 %copy-done.4 = bf16[6,48,128]{2,1,0:T(8,128)(2,1)S(1)} copy-done((bf16[6,48,128]{2,1,0:T(8,128)(2,1)S(1)}, bf16[6,48,128]{2,1,0:T(8,128)(2,1)}, u32[]{:S(2)}) %copy-start.4) | copy-done | bytes 73752
  17.4 0.0 copy-start.6
  17.4 0.8 %copy-done.6 = bf16[4,48,128]{2,1,0:T(8,128)(2,1)S(1)} copy-done((bf16[4,48,128]{2,1,0:T(8,128)(2,1)S(1)}, bf16[4,48,128]{2,1,0:T(8,128)(2,1)}, u32[]{:S(2)}) %copy-start.6) | copy-done | bytes 49176
  18.2 0.0 copy-start.7
  18.2 0.8 %copy-done.7 = bf16[4,48,128]{2,1,0:T(8,128)(2,1)S(1)} copy-done((bf16[4,48,128]{2,1,0:T(8,128)(2,1)S(1)}, bf16[4,48,128]{2,1,0:T(8,128)(2,1)}, u32[]{:S(2)}) %copy-start.7) | copy-done | bytes 49176
  19.0 11.1 %compute.1 = (f32[3,8,16,128]{3,2,1,0:T(8,128)}, bf16[16,16,128]{2,1,0:T(8,128)(2,1)S(1)}, f32[64,128]{1,0:T(8,128)S(1)}) custom-call(s32[8]{0:T(128)S(1)} %slice.3.fold, f32[3,8,16,128]{3,2,1,0:T(8,128)S(1)} %copy-done, f32[8,16,128]{2,1,0:T(8,128)S(1)} %copy-done.2, s32[16,128]{1,0:T(8,128)S(1)} %copy-done.8, bf16[16,16,128]{2,1,0:T(8,128)(2,1)S(1)} %bitcast.22, ...), custom_call_target="tpu_custom_call" | custom-call | tf_op jit(solution)/shard_map/compute/pallas_call | solution.py:510
  30.2 0.0 copy-start.9
  30.2 0.6 %copy-done.9 = f32[64,128]{1,0:T(8,128)} copy-done((f32[64,128]{1,0:T(8,128)}, f32[64,128]{1,0:T(8,128)S(1)}, u32[]{:S(2)}) %copy-start.9) | copy-done | bytes 32792
  30.8 0.6 %copy.23 = bf16[16,16,128]{2,1,0:T(8,128)(2,1)} copy(bf16[16,16,128]{2,0,1:T(8,128)(2,1)S(1)} %bitcast.24) | data formatting | bytes 131072
  31.4 15.1 %reduce.1 = f32[8,8,128]{2,1,0:T(8,128)} custom-call(f32[8,8,128]{2,1,0:T(8,128)} %bitcast.25), custom_call_target="tpu_custom_call" | custom-call | tf_op jit(solution)/shard_map/reduce/pallas_call | solution.py:535
  46.5 1.4 %copy.29 = f32[8192]{0:T(1024)} copy(f32[8192]{0:T(1024)} %bitcast.29) | data formatting | bytes 65536
  (3 shorter events, 0.1 us)
Async XLA Ops:
  0.6 0.8 %copy-start.5 = (bf16[64,64]{1,0:T(8,128)(2,1)S(1)}, bf16[64,64]{1,0:T(8,128)(2,1)}, u32[]{:S(2)}) copy-start(bf16[64,64]{1,0:T(8,128)(2,1)} %w_mix.1) | copy-start | bytes 24580
  2.4 0.8 %copy-start.10 = (bf16[9,16,64]{2,1,0:T(8,128)(2,1)S(1)}, bf16[9,16,64]{2,1,0:T(8,128)(2,1)}, u32[]{:S(2)}) copy-start(bf16[9,16,64]{2,1,0:T(8,128)(2,1)} %param.15) | copy-start | bytes 55300
  3.3 0.8 %copy-start.11 = (bf16[16,16,128]{2,1,0:T(8,128)(2,1)S(1)}, bf16[16,16,128]{2,1,0:T(8,128)(2,1)}, u32[]{:S(2)}) copy-start(bf16[16,16,128]{2,1,0:T(8,128)(2,1)} %param.16) | copy-start | bytes 196612
  4.1 0.8 %copy-start.12 = (s32[8192]{0:T(1024)S(1)}, s32[8192]{0:T(1024)}, u32[]{:S(2)}) copy-start(s32[8192]{0:T(1024)} %param.17) | copy-start | bytes 98308
  5.1 10.5 %copy-start = (f32[3,8,16,128]{3,2,1,0:T(8,128)S(1)}, f32[3,8,16,128]{3,2,1,0:T(8,128)}, u32[]{:S(2)}) copy-start(f32[3,8,16,128]{3,2,1,0:T(8,128)} %ocean.3) | copy-start | bytes 589828
  5.1 10.5 %copy-start.1 = (bf16[16,16,128]{2,0,1:T(8,128)(2,1)S(1)}, bf16[16,16,128]{2,0,1:T(8,128)(2,1)}, u32[]{:S(2)}) copy-start(bf16[16,16,128]{2,0,1:T(8,128)(2,1)} %copy.26) | copy-start | bytes 196612
  5.1 10.5 %copy-start.2 = (f32[8,16,128]{2,1,0:T(8,128)S(1)}, f32[8,16,128]{2,1,0:T(8,128)}, u32[]{:S(2)}) copy-start(f32[8,16,128]{2,1,0:T(8,128)} %kappa.3) | copy-start | bytes 196612
  5.1 10.5 %copy-start.8 = (s32[16,128]{1,0:T(8,128)S(1)}, s32[16,128]{1,0:T(8,128)}, u32[]{:S(2)}) copy-start(s32[16,128]{1,0:T(8,128)} %depth.3) | copy-start | bytes 24580
  15.6 0.9 %copy-start.3 = (bf16[8,2,48,128]{3,2,1,0:T(8,128)(2,1)S(1)}, bf16[8,2,48,128]{3,2,1,0:T(8,128)(2,1)}, u32[]{:S(2)}) copy-start(bf16[8,2,48,128]{3,2,1,0:T(8,128)(2,1)} %get-tuple-element.13.tops) | copy-start | bytes 589828
  16.6 0.9 %copy-start.4 = (bf16[6,48,128]{2,1,0:T(8,128)(2,1)S(1)}, bf16[6,48,128]{2,1,0:T(8,128)(2,1)}, u32[]{:S(2)}) copy-start(bf16[6,48,128]{2,1,0:T(8,128)(2,1)} %get-tuple-element.12.sides) | copy-start | bytes 221188
  17.4 0.8 %copy-start.6 = (bf16[4,48,128]{2,1,0:T(8,128)(2,1)S(1)}, bf16[4,48,128]{2,1,0:T(8,128)(2,1)}, u32[]{:S(2)}) copy-start(bf16[4,48,128]{2,1,0:T(8,128)(2,1)} %get-tuple-element.10.north) | copy-start | bytes 147460
  18.2 0.8 %copy-start.7 = (bf16[4,48,128]{2,1,0:T(8,128)(2,1)S(1)}, bf16[4,48,128]{2,1,0:T(8,128)(2,1)}, u32[]{:S(2)}) copy-start(bf16[4,48,128]{2,1,0:T(8,128)(2,1)} %get-tuple-element.11.south) | copy-start | bytes 147460
  30.2 0.6 %copy-start.9 = (f32[64,128]{1,0:T(8,128)}, f32[64,128]{1,0:T(8,128)S(1)}, u32[]{:S(2)}) copy-start(f32[64,128]{1,0:T(8,128)S(1)} %get-tuple-element.16) | copy-start | bytes 98308

commit v2 on v1

--- a/solution.py
+++ b/solution.py
@@ -24,13 +24,45 @@
     t = ocean[2, :, row, :] * wet
     k = kappa[:, row, :] * wet
     wet2 = jnp.concatenate([wet, wet], axis=0)
-    g = scale * wet2 * cot[row].astype(F32)
+    g = scale * wet2 * cot[:, row, :]
     return u, v, t, k, g, wet2
 
 
-def exchange_kernel(
-    n_lon, n_lat, scale, ocean, kappa, depth, cot, north, south, sides, tops,
-    rows, packed, top_own, row_send, row_recv, side_send, side_recv, top_send, top_recv,
+def dot(a, b):
+    return jnp.dot(a, b, preferred_element_type=F32)
+
+
+def dot_cells(a, b):
+    return lax.dot_general(a, b, (((1,), (1,)), ((), ())), preferred_element_type=F32)
+
+
+def slope(pre, sigma):
+    return sigma * (1.0 + pre * (1.0 - sigma))
+
+
+def sigmoid(pre):
+    return 1.0 / (1.0 + jnp.exp(-pre))
+
+
+def east_of(own, rim, lane):
+    a = pltpu.roll(own, 127, axis=own.ndim - 1)
+    b = pltpu.roll(rim, 127, axis=own.ndim - 1)
+    return jnp.where(lane == 127, b, a), jnp.where(lane == 127, a, b)
+
+
+def west_of(own, rim, lane):
+    a = pltpu.roll(own, 1, axis=own.ndim - 1)
+    b = pltpu.roll(rim, 1, axis=own.ndim - 1)
+    return jnp.where(lane == 0, b, a), jnp.where(lane == 0, a, b)
+
+
+def kernel(
+    n_lon, n_lat, scale, fold, ocean, kappa, depth, cot_in, first_w, mix_w, last_w, krow, klane, coriolis,
+    state, closure, out,
+    cot, closing, north, south, sides, tops, rows, packed, partner_pick, picks, w_first, w_last, w_back, w_mix_t,
+    f_a, f_b, h_a, h_b, ks_a, ks_b, g_own, wet2s, patches, slope1, slope2, hid1, hid2, hshift, gpatch, dmix, dfirst, table,
+    picked, got_lon, got_lat, chunk,
+    row_send, row_recv, side_send, side_recv, top_send, top_recv, out_sem1, in_sem1, out_sem2, in_sem2, out_sem3, in_sem3,
 ):
     lon = lax.axis_index("lon")
     lat = lax.axis_index("lat")
@@ -48,28 +80,35 @@
 
     for step in range(1, n_lon):
         greet(lat, lax.rem(lon + step, n_lon))
+    for step in range(1, n_lat):
+        greet(lax.rem(lat + step, n_lat), lon)
+    cot[...] = cot_in[...].astype(F32)
 
     @pl.when(has_north)
     def _():
-        for to in (lon, east, west):
+        for to in (east, west):
             greet(lat + 1, to)
 
     @pl.when(has_south)
     def _():
-        for to in (lon, east, west):
+        for to in (east, west):
             greet(lat - 1, to)
 
     lanes = lax.broadcasted_iota(jnp.int32, (48, 128), 1)
     acc = jnp.zeros((48, 128), F32)
     for row in range(count):
-        u, v, t, k, g, _ = masked_row(ocean, kappa, depth, cot, row, scale)
+        u, v, t, k, g, wet2 = masked_row(ocean, kappa, depth, cot, row, scale)
         line = jnp.concatenate([u, v, t, k, g], axis=0)
+        for f, field in enumerate((u, v, t, k)):
+            f_a[row + WIDE, f] = field
+        g_own[row + 1, 0] = g.astype(BF16).astype(F32)
+        wet2s[row] = wet2
         rows[row] = line.astype(BF16)
         acc = jnp.where(lanes // 8 == row, pltpu.roll(line, (4 + 8 * row) % 128, axis=1), acc)
     packed[...] = acc.astype(BF16)
 
     sides_open = has_north.astype(jnp.int32) + has_south.astype(jnp.int32)
-    pl.semaphore_wait(barrier, n_lon - 1 + 3 * sides_open)
+    pl.semaphore_wait(barrier, n_lon + n_lat - 2 + 2 * sides_open)
 
     def send_rows(start, dst, slot, to_lat):
         return pltpu.make_async_remote_copy(
@@ -128,6 +167,40 @@
         for copy in down:
             copy.start()
 
+
+    def placed(height, width, shift):
+        at = lax.broadcasted_iota(jnp.int32, (height, width), 0)
+        to = lax.broadcasted_iota(jnp.int32, (height, width), 1)
+        return jnp.where(at + shift == to, 1.0, 0.0).astype(BF16)
+
+    wide_w = dot(first_w[0], placed(24, 224, 0))
+    for k in range(1, 9):
+        wide_w += dot(first_w[k], placed(24, 224, 24 * k))
+    w_first[...] = wide_w.astype(BF16)
+    for k in range(3):
+        w_last[k] = sum(dot(last_w[3 * k + i], placed(64, 192, 64 * i)) for i in range(3)).astype(BF16)
+    back_w = jnp.concatenate([last_w[k].astype(F32) for k in range(9)], axis=0)
+    w_back[...] = back_w.T.astype(BF16)
+    w_mix_t[...] = mix_w[...].astype(F32).T.astype(BF16)
+    at_row = lax.broadcasted_iota(jnp.int32, (256, 128), 0)
+    at_lane = lax.broadcasted_iota(jnp.int32, (128, 128), 0)
+    for j in range(krow.shape[0]):
+        picks[:, 128 * j : 128 * j + 128] = jnp.where(at_row == krow[j : j + 1, :], 1.0, 0.0).astype(BF16)
+
+    @pl.when(at_top)
+    def _():
+        nx = n_lon * 128
+        s = fold[0]
+        at = lax.broadcasted_iota(jnp.int32, (128, 256), 0)
+        pos = lax.broadcasted_iota(jnp.int32, (1, 256), 1)
+        col = lon * 128 + jnp.where(pos >= 192, pos - 256, pos)
+        col = jnp.where(col < 0, col + nx, col)
+        col = jnp.where(col >= nx, col - nx, col)
+        partner = s - col
+        partner = jnp.where(partner < 0, partner + nx, partner)
+        for j in range(n_lon):
+            partner_pick[j] = jnp.where(at + 128 * j == partner, 1.0, 0.0).astype(BF16)
+
     for copy in same:
         copy.wait()
 
@@ -156,46 +229,7 @@
             send_top(step).wait_send()
             top_from(step).wait_recv()
 
-
-def dot(a, b):
-    return jnp.dot(a, b, preferred_element_type=F32)
-
-
-def dot_cells(a, b):
-    return lax.dot_general(a, b, (((1,), (1,)), ((), ())), preferred_element_type=F32)
-
-
-def slope(pre, sigma):
-    return sigma * (1.0 + pre * (1.0 - sigma))
-
-
-def sigmoid(pre):
-    return 1.0 / (1.0 + jnp.exp(-pre))
-
-
-def east_of(own, rim, lane):
-    a = pltpu.roll(own, 127, axis=own.ndim - 1)
-    b = pltpu.roll(rim, 127, axis=own.ndim - 1)
-    return jnp.where(lane == 127, b, a), jnp.where(lane == 127, a, b)
-
-
-def west_of(own, rim, lane):
-    a = pltpu.roll(own, 1, axis=own.ndim - 1)
-    b = pltpu.roll(rim, 1, axis=own.ndim - 1)
-    return jnp.where(lane == 0, b, a), jnp.where(lane == 0, a, b)
-
-
-def compute_kernel(
-    n_lon, n_lat, scale, fold, ocean, kappa, depth, cot, north, south, sides, tops,
-    w_first, w_mix, w_mix_t, w_last, w_back, krow, klane, coriolis,
-    state, closure, picked,
-    f_a, f_b, h_a, h_b, ks_a, ks_b, g_own, wet2s, patches, slope1, slope2, hid1, hid2, hshift, gpatch, dmix, dfirst, table,
-):
-    lon = lax.axis_index("lon")
-    lat = lax.axis_index("lat")
-    count = ocean.shape[2]
     total = count + 2 * WIDE
-    at_top = lat == n_lat - 1
     at_bottom = lat == 0
     lane = lax.broadcasted_iota(jnp.int32, (8, 128), 1)
     level = lax.broadcasted_iota(jnp.int32, (8, 128), 0)
@@ -223,30 +257,17 @@
     below = jnp.where(at_bottom, zero48, merge(2))
     above = jnp.where(at_top, zero48, merge(4))
     for row in range(count):
-        u, v, t, k, g, wet2 = masked_row(ocean, kappa, depth, cot, row, scale)
-        own = jnp.concatenate([u, v, t, k, g.astype(BF16).astype(F32)], axis=0)
-        put(row + WIDE, own, unpack(mid, row))
-        wet2s[row] = wet2
+        put(row + WIDE, None, unpack(mid, row))
     for row in range(WIDE):
         put(row, jnp.where(at_bottom, zero48, south[row].astype(F32)), unpack(below, count - WIDE + row))
         put(WIDE + count + row, jnp.where(at_top, zero48, north[row].astype(F32)), unpack(above, row))
 
     @pl.when(at_top)
     def _():
-        nx = n_lon * 128
-        s = fold[0]
-        at = lax.broadcasted_iota(jnp.int32, (128, 256), 0)
-        pos = lax.broadcasted_iota(jnp.int32, (1, 256), 1)
-        col = lon * 128 + jnp.where(pos >= 192, pos - 256, pos)
-        col = jnp.where(col < 0, col + nx, col)
-        col = jnp.where(col >= nx, col - nx, col)
-        partner = s - col
-        partner = jnp.where(partner < 0, partner + nx, partner)
         res = jnp.zeros((64, 256), F32)
         for j in range(n_lon):
-            pick = jnp.where(at + 128 * j == partner, 1.0, 0.0).astype(BF16)
             both = jnp.concatenate([tops[j, 1, 0:32], tops[j, 0, 0:32]], axis=0)
-            res = res + dot(both, pick)
+            res = res + dot(both, partner_pick[j])
         for q in range(2):
             for f in range(4):
                 sign = -1.0 if f < 2 else 1.0
@@ -305,9 +326,6 @@
 
     lax.fori_loop(1, total - 1, step(f_a, f_b, h_a, h_b), 0, unroll=2)
     lax.fori_loop(2, total - 2, step(h_a, h_b, f_a, f_b), 0, unroll=2)
-    for row in range(count):
-        for f in range(3):
-            state[f, :, row, :] = f_a[row + WIDE, f]
 
     lane24 = lax.broadcasted_iota(jnp.int32, (24, 128), 1)
     lane72 = lax.broadcasted_iota(jnp.int32, (72, 128), 1)
@@ -339,7 +357,7 @@
         pre1 = dot(w_first[...], patches[:, start : start + 256])
         s1 = sigmoid(pre1)
         h1 = (pre1 * s1).astype(BF16)
-        pre2 = dot(w_mix[...], h1)
+        pre2 = dot(mix_w[...], h1)
         s2 = sigmoid(pre2)
         hid1[:, start : start + 256] = h1
         hid2[:, start : start + 256] = (pre2 * s2).astype(BF16).astype(F32)
@@ -373,12 +391,6 @@
     for start in range(0, cells, 256):
         here = slice(start, start + 256)
         near = slice(start + 128, start + 384)
-        out = dot(w_last[0], hshift[:, start : start + 256])
-        out += dot(w_last[1], hshift[:, start + 128 : start + 384])
-        out += dot(w_last[2], hshift[:, start + 256 : start + 512])
-        for j in range(2):
-            r = start // 128 + j
-            closure[r] = (wet2s[r] * out[:, 128 * j : 128 * j + 128]).astype(BF16)
         back = dot(w_back[...], gpatch[:, here])
         dm = (back * slope2[:, near]).astype(BF16)
         dmix[:, here] = dm
@@ -400,58 +412,56 @@
     hi = q.astype(BF16)
     lo = (q - hi.astype(F32)).astype(BF16)
     split = jnp.concatenate([hi, lo], axis=0)
-    at_row = lax.broadcasted_iota(jnp.int32, (256, 128), 0)
-    at_lane = lax.broadcasted_iota(jnp.int32, (128, 128), 0)
+    per = picked.shape[1]
     for j in range(0, krow.shape[0], 2):
-        pick = jnp.concatenate(
-            [jnp.where(at_row == krow[j + i : j + i + 1, :], 1.0, 0.0).astype(BF16) for i in range(2)], axis=1
-        )
-        got = dot(split, pick)
+        got = dot(split, picks[:, 128 * j : 128 * j + 256])
         got = got[:128] + got[128:]
         for i in range(2):
             mine = jnp.where(at_lane == klane[j + i : j + i + 1, :], got[:, 128 * i : 128 * i + 128], 0.0)
-            picked[j + i : j + i + 1, :] = jnp.sum(mine, axis=0, keepdims=True)
-
-
-def reduce_kernel(n_lon, n_lat, part, out, got_lon, got_lat, chunk, s1, r1, s2, r2, s3, r3):
-    lon = lax.axis_index("lon")
-    lat = lax.axis_index("lat")
-    barrier = pltpu.get_barrier_semaphore()
+            to = (j + i) // per
+            picked[to, (j + i) % per : (j + i) % per + 1, :] = jnp.sum(mine, axis=0, keepdims=True)
+
     lons = [lax.rem(lon + step, n_lon) for step in range(1, n_lon)]
     lats = [lax.rem(lat + step, n_lat) for step in range(1, n_lat)]
-    for to in lons:
-        pl.semaphore_signal(barrier, inc=1, device_id=(to, lat), device_id_type=MESH)
-    for to in lats:
-        pl.semaphore_signal(barrier, inc=1, device_id=(lon, to), device_id_type=MESH)
-    pl.semaphore_wait(barrier, n_lon + n_lat - 2)
-
-    def copy(src, dst, ssem, rsem, to):
+    def share(src, dst, ssem, rsem, to):
         return pltpu.make_async_remote_copy(
             src_ref=src, dst_ref=dst, send_sem=ssem, recv_sem=rsem, device_id=to, device_id_type=MESH
         )
 
-    first = [copy(part.at[to], got_lon.at[lon], s1.at[to], r1.at[lon], (to, lat)) for to in lons]
+    first = [share(picked.at[to], got_lon.at[lon], out_sem1.at[to], in_sem1.at[lon], (to, lat)) for to in lons]
     for c in first:
         c.start()
-    got_lon[lon] = part[lon]
+    got_lon[lon] = picked[lon]
+
+    for start in range(0, cells, 256):
+        tend = dot(w_last[0], hshift[:, start : start + 256])
+        tend += dot(w_last[1], hshift[:, start + 128 : start + 384])
+        tend += dot(w_last[2], hshift[:, start + 256 : start + 512])
+        for j in range(2):
+            r = start // 128 + j
+            closing[:, r, :] = wet2s[r] * tend[:, 128 * j : 128 * j + 128]
+    closure[...] = closing[...].astype(BF16)
+    for row in range(count):
+        for f in range(3):
+            state[f, :, row, :] = f_a[row + WIDE, f]
     for c, to in zip(first, lons):
         c.wait_send()
-        copy(part.at[to], got_lon.at[to], s1.at[to], r1.at[to], (to, lat)).wait_recv()
+        share(picked.at[to], got_lon.at[to], out_sem1.at[to], in_sem1.at[to], (to, lat)).wait_recv()
     got_lat[lat] = jnp.sum(got_lon[...], axis=0)
-    second = [copy(got_lat.at[lat], got_lat.at[lat], s2.at[to], r2.at[lat], (lon, to)) for to in lats]
+    second = [share(got_lat.at[lat], got_lat.at[lat], out_sem2.at[to], in_sem2.at[lat], (lon, to)) for to in lats]
     for c in second:
         c.start()
     for c, to in zip(second, lats):
         c.wait_send()
-        copy(got_lat.at[to], got_lat.at[to], s2.at[to], r2.at[to], (lon, to)).wait_recv()
+        share(got_lat.at[to], got_lat.at[to], out_sem2.at[to], in_sem2.at[to], (lon, to)).wait_recv()
     chunk[...] = jnp.sum(got_lat[...], axis=0)
-    third = [copy(chunk, out.at[lon], s3.at[to], r3.at[lon], (to, lat)) for to in lons]
+    third = [share(chunk, out.at[lon], out_sem3.at[to], in_sem3.at[lon], (to, lat)) for to in lons]
     for c in third:
         c.start()
     out[lon] = chunk[...]
     for c, to in zip(third, lons):
         c.wait_send()
-        copy(chunk, out.at[to], s3.at[to], r3.at[to], (to, lat)).wait_recv()
+        share(chunk, out.at[to], out_sem3.at[to], in_sem3.at[to], (to, lat)).wait_recv()
 
 
 def entry_place(index):
@@ -477,74 +487,53 @@
     count = ocean_state.shape[2]
     row_total = count * n_lat
     scale = 1.0 / math.sqrt(row_total * 128 * n_lon)
-    cot = jnp.transpose(cotangent, (1, 0, 2))
     sds = jax.ShapeDtypeStruct
     dma = pltpu.SemaphoreType.DMA
-    north, south, sides, tops = pl.pallas_call(
-        functools.partial(exchange_kernel, n_lon, n_lat, scale),
-        out_shape=[
-            sds((WIDE, 48, 128), BF16), sds((WIDE, 48, 128), BF16), sds((6, 48, 128), BF16),
-            sds((n_lon, 2, 48, 128), BF16),
-        ],
-        in_specs=[VMEM] * 4,
-        out_specs=[VMEM] * 4,
-        scratch_shapes=[
-            pltpu.VMEM((count, 48, 128), BF16), pltpu.VMEM((48, 128), BF16), pltpu.VMEM((2, 48, 128), BF16),
-            dma((2,)), dma((2,)), dma((6,)), dma((6,)), dma((n_lon,)), dma((n_lon,)),
-        ],
-        compiler_params=pltpu.CompilerParams(collective_id=0, has_side_effects=True),
-        name="exchange",
-    )(ocean_state, diffusivity, depth_levels, cot)
-
+    vmem = pltpu.VMEM
     row_ids = lax.axis_index("lat") * count - WIDE + jnp.arange(count + 2 * WIDE, dtype=jnp.int32)
     mirrored = jnp.where(row_ids >= row_total, 2 * row_total - 1 - row_ids, row_ids)
     rows_f = 0.25 * jnp.sin(math.pi * (mirrored.astype(F32) + 0.5) / row_total - 0.5 * math.pi)
-    w_first = jnp.pad(jnp.transpose(first_weight, (1, 0, 2)).reshape(64, 216), ((0, 0), (0, 8)))
-    w_last = jnp.transpose(last_weight.reshape(3, 3, 16, 64), (0, 2, 1, 3)).reshape(3, 16, 192)
-    w_back = jnp.transpose(last_weight, (2, 0, 1)).reshape(64, 144)
     krow, klane = entry_place(active_index)
     picks = active_index.shape[0] // 128
+    depth = picks // n_lon
     total = count + 2 * WIDE
     wide = (count + 4) * 128
     cells = count * 128
-    state, closure, picked = pl.pallas_call(
-        functools.partial(compute_kernel, n_lon, n_lat, scale),
+    state, closure, reduced = pl.pallas_call(
+        functools.partial(kernel, n_lon, n_lat, scale),
         out_shape=[
-            sds((3, 8, count, 128), F32), sds((count, 16, 128), BF16), sds((picks, 128), F32),
+            sds((3, 8, count, 128), F32), sds((16, count, 128), BF16), sds((n_lon, depth, 128), F32),
         ],
-        in_specs=[SMEM] + [VMEM] * 15 + [SMEM],
+        in_specs=[SMEM] + [VMEM] * 9 + [SMEM],
         out_specs=[VMEM] * 3,
         scratch_shapes=[
-            pltpu.VMEM((total, 4, 8, 128), F32), pltpu.VMEM((total, 4, 8, 128), F32),
-            pltpu.VMEM((total, 3, 8, 128), F32), pltpu.VMEM((total, 3, 8, 128), F32),
-            pltpu.VMEM((total, 2, 8, 128), F32), pltpu.VMEM((total, 2, 8, 128), F32),
-            pltpu.VMEM((count + 2, 2, 16, 128), F32), pltpu.VMEM((count, 16, 128), F32),
-            pltpu.VMEM((224, wide), BF16), pltpu.VMEM((64, wide), F32), pltpu.VMEM((64, wide), F32),
-            pltpu.VMEM((64, wide), BF16), pltpu.VMEM((64, wide), F32), pltpu.VMEM((192, (count + 2) * 128), BF16),
-            pltpu.VMEM((144, cells), BF16), pltpu.VMEM((64, cells), BF16), pltpu.VMEM((64, cells), BF16),
-            pltpu.VMEM((256, 128), F32),
-        ],
-        compiler_params=pltpu.CompilerParams(vmem_limit_bytes=48 * 1024 * 1024),
-        name="compute",
-    )(
-        fold_pair[:8], ocean_state, diffusivity, depth_levels, cot, north, south, sides, tops, w_first, mix_weight,
-        mix_weight.T, w_last, w_back, krow.reshape(picks, 128), klane.reshape(picks, 128), rows_f,
-    )
-
-    depth = picks // n_lon
-    reduced = pl.pallas_call(
-        functools.partial(reduce_kernel, n_lon, n_lat),
-        out_shape=sds((n_lon, depth, 128), F32),
-        in_specs=[VMEM],
-        out_specs=VMEM,
-        scratch_shapes=[
-            pltpu.VMEM((n_lon, depth, 128), F32), pltpu.VMEM((n_lat, depth, 128), F32), pltpu.VMEM((depth, 128), F32),
+            vmem((16, count, 128), F32), vmem((16, count, 128), F32),
+            vmem((WIDE, 48, 128), BF16), vmem((WIDE, 48, 128), BF16), vmem((6, 48, 128), BF16),
+            vmem((n_lon, 2, 48, 128), BF16), vmem((count, 48, 128), BF16), vmem((48, 128), BF16),
+            vmem((n_lon, 128, 256), BF16), vmem((256, picks * 128), BF16),
+            vmem((64, 224), BF16), vmem((3, 16, 192), BF16), vmem((64, 144), BF16), vmem((64, 64), BF16),
+            vmem((total, 4, 8, 128), F32), vmem((total, 4, 8, 128), F32),
+            vmem((total, 3, 8, 128), F32), vmem((total, 3, 8, 128), F32),
+            vmem((total, 2, 8, 128), F32), vmem((total, 2, 8, 128), F32),
+            vmem((count + 2, 2, 16, 128), F32), vmem((count, 16, 128), F32),
+            vmem((224, wide), BF16), vmem((64, wide), F32), vmem((64, wide), F32),
+            vmem((64, wide), BF16), vmem((64, wide), F32), vmem((192, (count + 2) * 128), BF16),
+            vmem((144, cells), BF16), vmem((64, cells), BF16), vmem((64, cells), BF16),
+            vmem((256, 128), F32),
+            vmem((n_lon, depth, 128), F32), vmem((n_lon, depth, 128), F32), vmem((n_lat, depth, 128), F32),
+            vmem((depth, 128), F32),
+            dma((2,)), dma((2,)), dma((6,)), dma((6,)), dma((n_lon,)), dma((n_lon,)),
             dma((n_lon,)), dma((n_lon,)), dma((n_lat,)), dma((n_lat,)), dma((n_lon,)), dma((n_lon,)),
         ],
-        compiler_params=pltpu.CompilerParams(collective_id=1, has_side_effects=True),
-        name="reduce",
-    )(picked.reshape(n_lon, depth, 128))
-    return state, jnp.transpose(closure, (1, 0, 2)), reduced.reshape(-1)
+        compiler_params=pltpu.CompilerParams(
+            collective_id=0, has_side_effects=True, vmem_limit_bytes=48 * 1024 * 1024
+        ),
+        name="ocean",
+    )(
+        fold_pair, ocean_state, diffusivity, depth_levels, cotangent, first_weight, mix_weight, last_weight,
+        krow.reshape(picks, 128), klane.reshape(picks, 128), rows_f,
+    )
+    return state, closure, reduced.reshape(-1)
 
 
 def solution(mesh):

time: 48.6 us -> 36.4 us (0.75)
  Pallas kernels: 36.6 us -> 29.1 us
  local copies, waits for them, and re-layouts: 10.2 us -> 5.14 us
  other arithmetic: 0.28 us -> 1.07 us
    pallas_call x3 -> x1, Pallas kernels: 36.6 us -> 29.1 us  [on_device(): pl.pallas_call(functools.partial(kernel, n_lon, n_lat, scale), out_shape=...]
    unnamed x30 -> x18, local copies, waits for them, and re-layouts: 8.36 us -> 5.14 us
    reshape x4 -> x0, local copies, waits for them, and re-layouts: 1.11 us -> none  [the longest x1 0.9 us: on_device(): jnp.transpose(first_weight, (1, 0, 2)).reshape(64, 216)]
    reshape x1, other arithmetic: 0.23 us -> 1.02 us  [on_device(): klane.reshape(picks, 128)]
    slice x1 -> x0, local copies, waits for them, and re-layouts: 0.69 us -> none  [on_device(): fold_pair[:8]]
where the time goes in v2:
time: 36.4 us; the launch traced here: 36.1 us
  Pallas kernels  29.1 us (80%)
  local copies, waits for them, and re-layouts  5.14 us (14%)
  other arithmetic  1.07 us (3%)
  between operations  0.72 us (2%)
    pallas_call x1, Pallas kernels, on_device(): pl.pallas_call(functools.partial(kernel, n_lon, n_lat, scale), out_shape=...  29.1 us
    unnamed x18, local copies, waits for them, and re-layouts  5.14 us
    reshape x1, other arithmetic, on_device(): klane.reshape(picks, 128)  1.02 us

profile of v2, /device:TPU:0, one launch (start us, length us, event | category | flops | bytes accessed | tf_op | source)
XLA Modules:
  0.0 36.1 jit_solution(342082135772070054)
XLA Ops:
  0.6 0.0 copy-start
  0.7 1.0 %fusion.16 = (s32[64,128]{1,0:T(8,128)S(1)}, s32[64,128]{1,0:T(8,128)S(1)}) fusion(s32[8192]{0:T(1024)} %param.17), kind=kLoop, calls=%fused_computation.46 | loop fusion | flops 1196032 | bytes 98304 | tf_op jit(solution)/shard_map/reshape | solution.py:534
  1.7 0.0 copy-start.1
  1.7 0.0 copy-start.3
  1.7 0.0 copy-start.4
  1.8 1.0 %copy.12.first_w = bf16[9,64,24]{2,1,0:T(8,128)(2,1)S(1)} copy(bf16[9,64,24]{1,2,0:T(8,128)(2,1)} %param.13) | data formatting | bytes 55296 | tf_op args[4]
  2.7 0.0 copy-done
  2.7 0.0 copy-done.1
  2.8 0.0 copy-done.3
  2.8 0.0 copy-done.4
  2.8 0.0 copy-start.2
  2.8 0.8 %copy-done.2 = bf16[16,16,128]{2,1,0:T(8,128)(2,1)S(1)} copy-done((bf16[16,16,128]{2,1,0:T(8,128)(2,1)S(1)}, bf16[16,16,128]{2,1,0:T(8,128)(2,1)}, u32[]{:S(2)}) %copy-start.2) | copy-done | bytes 65560
  3.6 0.0 copy-start.5
  3.6 0.7 %copy-done.5 = s32[16,128]{1,0:T(8,128)S(1)} copy-done((s32[16,128]{1,0:T(8,128)S(1)}, s32[16,128]{1,0:T(8,128)}, u32[]{:S(2)}) %copy-start.5) | copy-done | bytes 8216
  4.3 0.0 copy-start.6
  4.3 0.7 %copy-done.6 = s32[1024]{0:T(1024)S(1)} copy-done((s32[1024]{0:T(1024)S(1)}, s32[1024]{0:T(1024)}, u32[]{:S(2)}) %copy-start.6) | copy-done | bytes 4120
  5.0 29.1 %ocean.2 = (f32[3,8,16,128]{3,2,1,0:T(8,128)S(1)}, bf16[16,16,128]{2,1,0:T(8,128)(2,1)S(1)}, f32[8,8,128]{2,1,0:T(8,128)S(1)}) custom-call(s32[1024]{0:T(1024)S(1)} %copy-done.6, f32[3,8,16,128]{3,2,1,0:T(8,128)S(1)} %copy-done, f32[8,16,128]{2,1,0:T(8,128)S(1)} %copy-done.1, s32[16,128]{1,0:T(8,128)S(1)} %copy-done.5, bf16[16,16,128]{2,1,0:T(8,128)(2,1)S(1)} %copy-done.2, ...), custom_call_target="tpu_custom_call" | custom-call | tf_op jit(solution)/shard_map/ocean/pallas_call | solution.py:502
  34.1 0.7 %copy.16 = f32[3,8,16,128]{3,2,1,0:T(8,128)} copy(f32[3,8,16,128]{3,2,1,0:T(8,128)S(1)} %get-tuple-element.14) | data formatting | bytes 393216
  34.8 0.6 %copy.17 = bf16[16,16,128]{2,1,0:T(8,128)(2,1)} copy(bf16[16,16,128]{2,1,0:T(8,128)(2,1)S(1)} %get-tuple-element.15) | data formatting | bytes 131072
  35.4 0.6 %copy.18 = f32[8192]{0:T(1024)} copy(f32[8192]{0:T(1024)S(1)} %bitcast.5) | data formatting | bytes 65536
  (1 shorter events, 0.0 us)
Async XLA Ops:
  0.6 2.1 %copy-start = (f32[3,8,16,128]{3,2,1,0:T(8,128)S(1)}, f32[3,8,16,128]{3,2,1,0:T(8,128)}, u32[]{:S(2)}) copy-start(f32[3,8,16,128]{3,2,1,0:T(8,128)} %ocean.3) | copy-start | bytes 589828
  1.7 1.0 %copy-start.1 = (f32[8,16,128]{2,1,0:T(8,128)S(1)}, f32[8,16,128]{2,1,0:T(8,128)}, u32[]{:S(2)}) copy-start(f32[8,16,128]{2,1,0:T(8,128)} %kappa.1) | copy-start | bytes 196612
  1.7 1.0 %copy-start.3 = (bf16[9,16,64]{2,1,0:T(8,128)(2,1)S(1)}, bf16[9,16,64]{2,1,0:T(8,128)(2,1)}, u32[]{:S(2)}) copy-start(bf16[9,16,64]{2,1,0:T(8,128)(2,1)} %last_w.1) | copy-start | bytes 55300
  1.7 1.0 %copy-start.4 = (bf16[64,64]{1,0:T(8,128)(2,1)S(1)}, bf16[64,64]{1,0:T(8,128)(2,1)}, u32[]{:S(2)}) copy-start(bf16[64,64]{1,0:T(8,128)(2,1)} %mix_w.1) | copy-start | bytes 24580
  2.8 0.8 %copy-start.2 = (bf16[16,16,128]{2,1,0:T(8,128)(2,1)S(1)}, bf16[16,16,128]{2,1,0:T(8,128)(2,1)}, u32[]{:S(2)}) copy-start(bf16[16,16,128]{2,1,0:T(8,128)(2,1)} %cot_in.1) | copy-start | bytes 196612
  3.6 0.7 %copy-start.5 = (s32[16,128]{1,0:T(8,128)S(1)}, s32[16,128]{1,0:T(8,128)}, u32[]{:S(2)}) copy-start(s32[16,128]{1,0:T(8,128)} %depth.1) | copy-start | bytes 24580
  4.3 0.7 %copy-start.6 = (s32[1024]{0:T(1024)S(1)}, s32[1024]{0:T(1024)}, u32[]{:S(2)}) copy-start(s32[1024]{0:T(1024)} %fold.1) | copy-start | bytes 12292

commit v3 on v2

--- a/solution.py
+++ b/solution.py
@@ -13,7 +13,8 @@
 BF16 = jnp.bfloat16
 WIDE = 4
 VMEM = pl.BlockSpec(memory_space=pltpu.VMEM)
-SMEM = pl.BlockSpec(memory_space=pltpu.SMEM)
+HBM = pl.BlockSpec(memory_space=pltpu.HBM)
+ANY = pl.BlockSpec(memory_space=pl.ANY)
 
 
 def masked_row(ocean, kappa, depth, cot, row, scale):
@@ -36,12 +37,16 @@
     return lax.dot_general(a, b, (((1,), (1,)), ((), ())), preferred_element_type=F32)
 
 
+def dot_first(a, b):
+    return lax.dot_general(a, b, (((0,), (0,)), ((), ())), preferred_element_type=F32)
+
+
 def slope(pre, sigma):
     return sigma * (1.0 + pre * (1.0 - sigma))
 
 
 def sigmoid(pre):
-    return 1.0 / (1.0 + jnp.exp(-pre))
+    return 0.5 + 0.5 * jnp.tanh(0.5 * pre)
 
 
 def east_of(own, rim, lane):
@@ -57,12 +62,24 @@
 
 
 def kernel(
-    n_lon, n_lat, scale, fold, ocean, kappa, depth, cot_in, first_w, mix_w, last_w, krow, klane, coriolis,
+    n_lon, n_lat, scale, *refs,
+):
+    operands, refs = refs[:9], refs[9:]
+    outputs, refs = refs[:3], refs[3:]
+    held, refs = refs[:9], refs[9:]
+    loads = [pltpu.make_async_copy(a, b, refs[0].at[i]) for i, (a, b) in enumerate(zip(operands, held))]
+    for i in (0, 1, 2, 3, 5, 6, 7, 8, 4):
+        loads[i].start()
+    ocean_step(n_lon, n_lat, scale, loads, *held, *outputs, *refs[1:])
+
+
+def ocean_step(
+    n_lon, n_lat, scale, loads, ocean, kappa, depth, cot_in, fold, first_w, mix_w, last_w, active,
     state, closure, out,
-    cot, closing, north, south, sides, tops, rows, packed, partner_pick, picks, w_first, w_last, w_back, w_mix_t,
+    krow, klane, coriolis, north_g, south_g, cot, closing, north, south, sides, tops, rows, packed, partner_pick, picks, w_first, w_last, w_back, w_mix_t,
     f_a, f_b, h_a, h_b, ks_a, ks_b, g_own, wet2s, patches, slope1, slope2, hid1, hid2, hshift, gpatch, dmix, dfirst, table,
     picked, got_lon, got_lat, chunk,
-    row_send, row_recv, side_send, side_recv, top_send, top_recv, out_sem1, in_sem1, out_sem2, in_sem2, out_sem3, in_sem3,
+    row_send, row_recv, g_send, g_recv, side_send, side_recv, top_send, top_recv, out_sem1, in_sem1, out_sem2, in_sem2, out_sem3, in_sem3,
 ):
     lon = lax.axis_index("lon")
     lat = lax.axis_index("lat")
@@ -82,7 +99,6 @@
         greet(lat, lax.rem(lon + step, n_lon))
     for step in range(1, n_lat):
         greet(lax.rem(lat + step, n_lat), lon)
-    cot[...] = cot_in[...].astype(F32)
 
     @pl.when(has_north)
     def _():
@@ -94,6 +110,9 @@
         for to in (east, west):
             greet(lat - 1, to)
 
+    for load in loads[:4]:
+        load.wait()
+    cot[...] = cot_in[...].astype(F32)
     lanes = lax.broadcasted_iota(jnp.int32, (48, 128), 1)
     acc = jnp.zeros((48, 128), F32)
     for row in range(count):
@@ -112,8 +131,14 @@
 
     def send_rows(start, dst, slot, to_lat):
         return pltpu.make_async_remote_copy(
-            src_ref=rows.at[pl.ds(start, WIDE)], dst_ref=dst, send_sem=row_send.at[slot],
+            src_ref=rows.at[pl.ds(start, WIDE), pl.ds(0, 32)], dst_ref=dst, send_sem=row_send.at[slot],
             recv_sem=row_recv.at[slot], device_id=(lon, to_lat), device_id_type=MESH,
+        )
+
+    def send_g(start, dst, slot, to_lat):
+        return pltpu.make_async_remote_copy(
+            src_ref=rows.at[start, pl.ds(32, 16)], dst_ref=dst, send_sem=g_send.at[slot],
+            recv_sem=g_recv.at[slot], device_id=(lon, to_lat), device_id_type=MESH,
         )
 
     def send_side(slot, to_lat, to_lon):
@@ -124,48 +149,52 @@
 
     def send_top(step):
         return pltpu.make_async_remote_copy(
-            src_ref=rows.at[pl.ds(count - 2, 2)], dst_ref=tops.at[lon], send_sem=top_send.at[step],
+            src_ref=rows.at[pl.ds(count - 2, 2), pl.ds(0, 32)], dst_ref=tops.at[lon], send_sem=top_send.at[step],
             recv_sem=top_recv.at[lon], device_id=(lax.rem(lon + step, n_lon), lat), device_id_type=MESH,
         )
 
     def top_from(step):
         peer = lax.rem(lon + step, n_lon)
         return pltpu.make_async_remote_copy(
-            src_ref=rows.at[pl.ds(count - 2, 2)], dst_ref=tops.at[peer], send_sem=top_send.at[step],
+            src_ref=rows.at[pl.ds(count - 2, 2), pl.ds(0, 32)], dst_ref=tops.at[peer], send_sem=top_send.at[step],
             recv_sem=top_recv.at[peer], device_id=(peer, lat), device_id_type=MESH,
         )
 
     to_north = send_rows(count - WIDE, south, 0, lat + 1)
     to_south = send_rows(0, north, 1, lat - 1)
+    g_north = send_g(count - 1, south_g, 0, lat + 1)
+    g_south = send_g(0, north_g, 1, lat - 1)
     same = [send_side(0, lat, east), send_side(1, lat, west)]
     up = [send_side(2, lat + 1, east), send_side(3, lat + 1, west)]
     down = [send_side(4, lat - 1, east), send_side(5, lat - 1, west)]
 
-    @pl.when(has_north)
-    def _():
-        to_north.start()
-
-    @pl.when(has_south)
-    def _():
-        to_south.start()
+    for copy in same:
+        copy.start()
 
     @pl.when(at_top)
     def _():
         for step in range(1, n_lon):
             send_top(step).start()
 
-    for copy in same:
-        copy.start()
+    @pl.when(has_north)
+    def _():
+        to_north.start()
+
+    @pl.when(has_south)
+    def _():
+        to_south.start()
 
     @pl.when(has_north)
     def _():
         for copy in up:
             copy.start()
+        g_north.start()
 
     @pl.when(has_south)
     def _():
         for copy in down:
             copy.start()
+        g_south.start()
 
 
     def placed(height, width, shift):
@@ -173,9 +202,17 @@
         to = lax.broadcasted_iota(jnp.int32, (height, width), 1)
         return jnp.where(at + shift == to, 1.0, 0.0).astype(BF16)
 
-    wide_w = dot(first_w[0], placed(24, 224, 0))
+    for load in loads[4:]:
+        load.wait()
+    first = lat * count - WIDE
+    row_total = count * n_lat
+    row_ids = first + lax.broadcasted_iota(jnp.int32, coriolis.shape, 0)
+    mirrored = jnp.where(row_ids >= row_total, 2 * row_total - 1 - row_ids, row_ids)
+    coriolis[...] = 0.25 * jnp.sin(math.pi * (mirrored.astype(F32) + 0.5) / row_total - 0.5 * math.pi)
+    krow[...], klane[...] = entry_place(active[...])
+    wide_w = dot_first(first_w[0], placed(24, 224, 0))
     for k in range(1, 9):
-        wide_w += dot(first_w[k], placed(24, 224, 24 * k))
+        wide_w += dot_first(first_w[k], placed(24, 224, 24 * k))
     w_first[...] = wide_w.astype(BF16)
     for k in range(3):
         w_last[k] = sum(dot(last_w[3 * k + i], placed(64, 192, 64 * i)) for i in range(3)).astype(BF16)
@@ -190,7 +227,7 @@
     @pl.when(at_top)
     def _():
         nx = n_lon * 128
-        s = fold[0]
+        s = fold[0:1, 0:1]
         at = lax.broadcasted_iota(jnp.int32, (128, 256), 0)
         pos = lax.broadcasted_iota(jnp.int32, (1, 256), 1)
         col = lon * 128 + jnp.where(pos >= 192, pos - 256, pos)
@@ -201,39 +238,12 @@
         for j in range(n_lon):
             partner_pick[j] = jnp.where(at + 128 * j == partner, 1.0, 0.0).astype(BF16)
 
-    for copy in same:
-        copy.wait()
-
-    @pl.when(has_north)
-    def _():
-        to_north.wait_send()
-        to_south.wait_recv()
-        for copy in up:
-            copy.wait_send()
-        for copy in down:
-            copy.wait_recv()
-
-    @pl.when(has_south)
-    def _():
-        to_south.wait_send()
-        to_north.wait_recv()
-        for copy in down:
-            copy.wait_send()
-        for copy in up:
-            copy.wait_recv()
-
-    @pl.when(at_top)
-    def _():
-        tops[lon] = rows[count - 2 : count]
-        for step in range(1, n_lon):
-            send_top(step).wait_send()
-            top_from(step).wait_recv()
-
     total = count + 2 * WIDE
     at_bottom = lat == 0
     lane = lax.broadcasted_iota(jnp.int32, (8, 128), 1)
     level = lax.broadcasted_iota(jnp.int32, (8, 128), 0)
     lane48 = lax.broadcasted_iota(jnp.int32, (48, 128), 1)
+    zero32 = jnp.zeros((32, 128), F32)
     zero48 = jnp.zeros((48, 128), F32)
 
     def merge(low):
@@ -246,34 +256,10 @@
                 f_a[row, f] = own[8 * f : 8 * f + 8]
             f_b[row, f] = rim[8 * f : 8 * f + 8]
         if WIDE - 1 <= row <= WIDE + count:
-            if own is not None:
-                g_own[row - WIDE + 1, 0] = own[32:48]
             g_own[row - WIDE + 1, 1] = rim[32:48]
 
     def unpack(side, row):
         return pltpu.roll(side, (128 - 4 - 8 * row) % 128, axis=1)
-
-    mid = merge(0)
-    below = jnp.where(at_bottom, zero48, merge(2))
-    above = jnp.where(at_top, zero48, merge(4))
-    for row in range(count):
-        put(row + WIDE, None, unpack(mid, row))
-    for row in range(WIDE):
-        put(row, jnp.where(at_bottom, zero48, south[row].astype(F32)), unpack(below, count - WIDE + row))
-        put(WIDE + count + row, jnp.where(at_top, zero48, north[row].astype(F32)), unpack(above, row))
-
-    @pl.when(at_top)
-    def _():
-        res = jnp.zeros((64, 256), F32)
-        for j in range(n_lon):
-            both = jnp.concatenate([tops[j, 1, 0:32], tops[j, 0, 0:32]], axis=0)
-            res = res + dot(both, partner_pick[j])
-        for q in range(2):
-            for f in range(4):
-                sign = -1.0 if f < 2 else 1.0
-                part = sign * res[32 * q + 8 * f : 32 * q + 8 * f + 8]
-                f_a[WIDE + count + q, f] = part[:, :128]
-                f_b[WIDE + count + q, f] = part[:, 128:]
 
     def roots(r, _):
         k_a, k_b = f_a[r, 3], f_b[r, 3]
@@ -284,8 +270,6 @@
         ks_b[r, 1] = jnp.sqrt(k_b * f_b[r + 1, 3])
         return 0
 
-    lax.fori_loop(0, total - 1, roots, 0, unroll=2)
-
     def summed(x):
         for d in (1, 2, 4):
             x = x + jnp.where(level >= d, pltpu.roll(x, d, axis=0), 0.0)
@@ -293,7 +277,7 @@
 
     def step(src_a, src_b, dst_a, dst_b):
         def body(r, _):
-            fr = coriolis[r]
+            fr = coriolis[pl.ds(r, 1), :]
             ke_a, ke_b = ks_a[r, 0], ks_b[r, 0]
             kw_a, kw_b = west_of(ke_a, ke_b, lane)
             coef = ((ke_a, kw_a, ks_a[r, 1], ks_a[r - 1, 1]), (ke_b, kw_b, ks_b[r, 1], ks_b[r - 1, 1]))
@@ -324,7 +308,71 @@
 
         return body
 
-    lax.fori_loop(1, total - 1, step(f_a, f_b, h_a, h_b), 0, unroll=2)
+    first_step = step(f_a, f_b, h_a, h_b)
+    for copy in same:
+        copy.wait()
+    mid = merge(0)
+    for row in range(count):
+        put(row + WIDE, None, unpack(mid, row))
+    low, high = WIDE, WIDE + count - 1
+    lax.fori_loop(low, high, roots, 0, unroll=3)
+    lax.fori_loop(low + 1, high, first_step, 0, unroll=2)
+
+    @pl.when(has_north)
+    def _():
+        to_north.wait_send()
+        to_south.wait_recv()
+        g_north.wait_send()
+        g_south.wait_recv()
+        for copy in up:
+            copy.wait_send()
+        for copy in down:
+            copy.wait_recv()
+
+    @pl.when(has_south)
+    def _():
+        to_south.wait_send()
+        to_north.wait_recv()
+        g_south.wait_send()
+        g_north.wait_recv()
+        for copy in down:
+            copy.wait_send()
+        for copy in up:
+            copy.wait_recv()
+
+    @pl.when(at_top)
+    def _():
+        tops[lon] = rows[count - 2 : count, 0:32]
+        for step in range(1, n_lon):
+            send_top(step).wait_send()
+            top_from(step).wait_recv()
+
+    below = jnp.where(at_bottom, zero48, merge(2))
+    above = jnp.where(at_top, zero48, merge(4))
+    for row in range(WIDE):
+        put(row, jnp.where(at_bottom, zero32, south[row].astype(F32)), unpack(below, count - WIDE + row))
+        put(WIDE + count + row, jnp.where(at_top, zero32, north[row].astype(F32)), unpack(above, row))
+
+    g_own[0, 0] = jnp.where(at_bottom, zero48[:16], south_g[...].astype(F32))
+    g_own[count + 1, 0] = jnp.where(at_top, zero48[:16], north_g[...].astype(F32))
+
+    @pl.when(at_top)
+    def _():
+        res = jnp.zeros((64, 256), F32)
+        for j in range(n_lon):
+            both = jnp.concatenate([tops[j, 1, 0:32], tops[j, 0, 0:32]], axis=0)
+            res = res + dot(both, partner_pick[j])
+        for q in range(2):
+            for f in range(4):
+                sign = -1.0 if f < 2 else 1.0
+                part = sign * res[32 * q + 8 * f : 32 * q + 8 * f + 8]
+                f_a[WIDE + count + q, f] = part[:, :128]
+                f_b[WIDE + count + q, f] = part[:, 128:]
+
+    lax.fori_loop(0, low, roots, 0, unroll=True)
+    lax.fori_loop(high, total - 1, roots, 0, unroll=True)
+    lax.fori_loop(1, low + 1, first_step, 0, unroll=2)
+    lax.fori_loop(high, total - 1, first_step, 0, unroll=2)
     lax.fori_loop(2, total - 2, step(h_a, h_b, f_a, f_b), 0, unroll=2)
 
     lane24 = lax.broadcasted_iota(jnp.int32, (24, 128), 1)
@@ -465,19 +513,32 @@
 
 
 def entry_place(index):
-    k, rest = index // 1536, index % 1536
-    col = (k * 24) + rest % 24
-    row_f, lane_f = rest // 24 + 64 * (col // 128), col % 128
+    def parts(value, size):
+        whole = jnp.floor((value.astype(F32) + 0.5) * (1.0 / size)).astype(jnp.int32)
+        return whole, value - size * whole
+
+    k, rest = parts(index, 1536)
+    o, c = parts(rest, 24)
+    col = k * 24 + c
+    row_f, lane_f = o + 64 * (col >> 7), col & 127
     m = index - 13824
-    row_m, lane_m = 128 + m // 64, m % 64
+    row_m, lane_m = 128 + (m >> 6), m & 63
     m = index - 17920
-    o, col = (m % 1024) // 64, (m // 1024) * 64 + m % 64
+    o, col = (m & 1023) >> 6, (m >> 10) * 64 + (m & 63)
     spill = col >= 512
-    row_l = jnp.where(spill, 128 + o, 192 + 16 * (col // 128) + o)
-    lane_l = jnp.where(spill, 64 + col - 512, col % 128)
+    row_l = jnp.where(spill, 128 + o, 192 + 16 * (col >> 7) + o)
+    lane_l = jnp.where(spill, 64 + col - 512, col & 127)
     row = jnp.where(index < 13824, row_f, jnp.where(index < 17920, row_m, row_l))
     lane = jnp.where(index < 13824, lane_f, jnp.where(index < 17920, lane_m, lane_l))
     return row, lane
+
+
+def store_kernel(*refs):
+    copies = [pltpu.make_async_copy(refs[i], refs[3 + i], refs[6].at[i]) for i in range(3)]
+    for copy in copies:
+        copy.start()
+    for copy in copies:
+        copy.wait()
 
 
 def on_device(
@@ -490,26 +551,29 @@
     sds = jax.ShapeDtypeStruct
     dma = pltpu.SemaphoreType.DMA
     vmem = pltpu.VMEM
-    row_ids = lax.axis_index("lat") * count - WIDE + jnp.arange(count + 2 * WIDE, dtype=jnp.int32)
-    mirrored = jnp.where(row_ids >= row_total, 2 * row_total - 1 - row_ids, row_ids)
-    rows_f = 0.25 * jnp.sin(math.pi * (mirrored.astype(F32) + 0.5) / row_total - 0.5 * math.pi)
-    krow, klane = entry_place(active_index)
     picks = active_index.shape[0] // 128
     depth = picks // n_lon
     total = count + 2 * WIDE
     wide = (count + 4) * 128
     cells = count * 128
-    state, closure, reduced = pl.pallas_call(
+    operands = (
+        ocean_state, diffusivity, depth_levels, cotangent, fold_pair.reshape(-1, 128),
+        jnp.transpose(first_weight, (0, 2, 1)), mix_weight, last_weight, active_index.reshape(picks, 128),
+    )
+    outs = [
+        sds((3, 8, count, 128), F32), sds((16, count, 128), BF16), sds((n_lon, depth, 128), F32),
+    ]
+    results = pl.pallas_call(
         functools.partial(kernel, n_lon, n_lat, scale),
-        out_shape=[
-            sds((3, 8, count, 128), F32), sds((16, count, 128), BF16), sds((n_lon, depth, 128), F32),
-        ],
-        in_specs=[SMEM] + [VMEM] * 9 + [SMEM],
+        out_shape=outs,
+        in_specs=[HBM] * 9,
         out_specs=[VMEM] * 3,
-        scratch_shapes=[
+        scratch_shapes=[vmem(x.shape, x.dtype) for x in operands] + [
+            dma((9,)), vmem((picks, 128), jnp.int32), vmem((picks, 128), jnp.int32), vmem((total, 128), F32),
+            vmem((16, 128), BF16), vmem((16, 128), BF16),
             vmem((16, count, 128), F32), vmem((16, count, 128), F32),
-            vmem((WIDE, 48, 128), BF16), vmem((WIDE, 48, 128), BF16), vmem((6, 48, 128), BF16),
-            vmem((n_lon, 2, 48, 128), BF16), vmem((count, 48, 128), BF16), vmem((48, 128), BF16),
+            vmem((WIDE, 32, 128), BF16), vmem((WIDE, 32, 128), BF16), vmem((6, 48, 128), BF16),
+            vmem((n_lon, 2, 32, 128), BF16), vmem((count, 48, 128), BF16), vmem((48, 128), BF16),
             vmem((n_lon, 128, 256), BF16), vmem((256, picks * 128), BF16),
             vmem((64, 224), BF16), vmem((3, 16, 192), BF16), vmem((64, 144), BF16), vmem((64, 64), BF16),
             vmem((total, 4, 8, 128), F32), vmem((total, 4, 8, 128), F32),
@@ -522,17 +586,22 @@
             vmem((256, 128), F32),
             vmem((n_lon, depth, 128), F32), vmem((n_lon, depth, 128), F32), vmem((n_lat, depth, 128), F32),
             vmem((depth, 128), F32),
-            dma((2,)), dma((2,)), dma((6,)), dma((6,)), dma((n_lon,)), dma((n_lon,)),
+            dma((2,)), dma((2,)), dma((2,)), dma((2,)), dma((6,)), dma((6,)), dma((n_lon,)), dma((n_lon,)),
             dma((n_lon,)), dma((n_lon,)), dma((n_lat,)), dma((n_lat,)), dma((n_lon,)), dma((n_lon,)),
         ],
         compiler_params=pltpu.CompilerParams(
             collective_id=0, has_side_effects=True, vmem_limit_bytes=48 * 1024 * 1024
         ),
         name="ocean",
-    )(
-        fold_pair, ocean_state, diffusivity, depth_levels, cotangent, first_weight, mix_weight, last_weight,
-        krow.reshape(picks, 128), klane.reshape(picks, 128), rows_f,
-    )
+    )(*operands)
+    state, closure, reduced = pl.pallas_call(
+        store_kernel,
+        out_shape=outs,
+        in_specs=[ANY] * 3,
+        out_specs=[ANY] * 3,
+        scratch_shapes=[dma((3,))],
+        name="store",
+    )(*results)
     return state, closure, reduced.reshape(-1)
 
 

time: 36.4 us -> 47.3 us (1.30)
  Pallas kernels: 29.1 us -> 37.2 us
  local copies, waits for them, and re-layouts: 5.14 us -> 8.92 us
  other arithmetic: 1.07 us -> 0 us
    pallas_call x0 -> x1, Pallas kernels: none -> 10.1 us  [on_device(): pl.pallas_call(store_kernel, out_shape=outs, in_specs=[ANY] * 3, out_spec...]
    unnamed x18 -> x24, local copies, waits for them, and re-layouts: 5.14 us -> 8.92 us
    pallas_call x1, Pallas kernels: 29.1 us -> 27.1 us  [on_device(): pl.pallas_call(functools.partial(kernel, n_lon, n_lat, scale), out_shape=...]
    reshape x1 -> x0, other arithmetic: 1.02 us -> none  [on_device(): klane.reshape(picks, 128)]
where the time goes in v3:
time: 47.3 us; the launch traced here: 46.8 us
  Pallas kernels  37.2 us (79%)
  local copies, waits for them, and re-layouts  8.92 us (19%)
  between operations  0.67 us (1%)
    pallas_call x1, Pallas kernels, on_device(): pl.pallas_call(functools.partial(kernel, n_lon, n_lat, scale), out_shape=...  27.1 us
    pallas_call x1, Pallas kernels, on_device(): pl.pallas_call(store_kernel, out_shape=outs, in_specs=[ANY] * 3, out_spec...  10.1 us
    unnamed x24, local copies, waits for them, and re-layouts  8.92 us

profile of v3, /device:TPU:0, one launch (start us, length us, event | category | flops | bytes accessed | tf_op | source)
XLA Modules:
  0.0 46.8 jit_solution(17517152347260246144)
XLA Ops:
  0.6 0.0 copy-start.11
  0.6 0.7 %copy-done.11 = s32[1024]{0:T(1024)S(1)} copy-done((s32[1024]{0:T(1024)S(1)}, s32[1024]{0:T(1024)}, u32[]{:S(2)}) %copy-start.11) | copy-done | bytes 4120
  1.3 0.0 copy-start.1
  1.3 0.9 %copy-done.1 = f32[3,8,16,128]{3,2,1,0:T(8,128)S(1)} copy-done((f32[3,8,16,128]{3,2,1,0:T(8,128)S(1)}, f32[3,8,16,128]{3,2,1,0:T(8,128)}, u32[]{:S(2)}) %copy-start.1) | copy-done | bytes 196632
  2.2 0.0 copy-start.3
  2.3 0.8 %copy-done.3 = f32[8,16,128]{2,1,0:T(8,128)S(1)} copy-done((f32[8,16,128]{2,1,0:T(8,128)S(1)}, f32[8,16,128]{2,1,0:T(8,128)}, u32[]{:S(2)}) %copy-start.3) | copy-done | bytes 65560
  3.1 0.0 copy-start.4
  3.1 0.8 %copy-done.4 = bf16[16,16,128]{2,1,0:T(8,128)(2,1)S(1)} copy-done((bf16[16,16,128]{2,1,0:T(8,128)(2,1)S(1)}, bf16[16,16,128]{2,1,0:T(8,128)(2,1)}, u32[]{:S(2)}) %copy-start.4) | copy-done | bytes 65560
  3.9 0.0 copy-start.5
  3.9 0.8 %copy-done.5 = bf16[9,64,24]{1,2,0:T(8,128)(2,1)S(1)} copy-done((bf16[9,64,24]{1,2,0:T(8,128)(2,1)S(1)}, bf16[9,64,24]{1,2,0:T(8,128)(2,1)}, u32[]{:S(2)}) %copy-start.5) | copy-done | bytes 27672
  4.7 0.0 copy-start.6
  4.7 0.8 %copy-done.6 = bf16[9,16,64]{2,1,0:T(8,128)(2,1)S(1)} copy-done((bf16[9,16,64]{2,1,0:T(8,128)(2,1)S(1)}, bf16[9,16,64]{2,1,0:T(8,128)(2,1)}, u32[]{:S(2)}) %copy-start.6) | copy-done | bytes 18456
  5.5 0.0 copy-start.8
  5.5 0.8 %copy-done.8 = s32[8192]{0:T(1024)S(1)} copy-done((s32[8192]{0:T(1024)S(1)}, s32[8192]{0:T(1024)}, u32[]{:S(2)}) %copy-start.8) | copy-done | bytes 32792
  6.3 0.0 copy-start.9
  6.3 0.7 %copy-done.9 = bf16[64,64]{1,0:T(8,128)(2,1)S(1)} copy-done((bf16[64,64]{1,0:T(8,128)(2,1)S(1)}, bf16[64,64]{1,0:T(8,128)(2,1)}, u32[]{:S(2)}) %copy-start.9) | copy-done | bytes 8216
  7.0 0.0 copy-start.10
  7.0 0.7 %copy-done.10 = s32[16,128]{1,0:T(8,128)S(1)} copy-done((s32[16,128]{1,0:T(8,128)S(1)}, s32[16,128]{1,0:T(8,128)}, u32[]{:S(2)}) %copy-start.10) | copy-done | bytes 8216
  7.7 27.1 %ocean.1 = (f32[3,8,16,128]{3,2,1,0:T(8,128)S(1)}, bf16[16,16,128]{2,1,0:T(8,128)(2,1)S(1)}, f32[8,8,128]{2,1,0:T(8,128)S(1)}) custom-call(f32[3,8,16,128]{3,2,1,0:T(8,128)S(1)} %copy-done.1, f32[8,16,128]{2,1,0:T(8,128)S(1)} %copy-done.3, s32[16,128]{1,0:T(8,128)S(1)} %copy-done.10, bf16[16,16,128]{2,1,0:T(8,128)(2,1)S(1)} %copy-done.4, ...), custom_call_target="tpu_custom_call" | custom-call | tf_op jit(solution)/shard_map/ocean/pallas_call | solution.py:566
  34.8 0.0 copy-start
  34.8 0.7 %copy-done = f32[3,8,16,128]{3,2,1,0:T(8,128)} copy-done((f32[3,8,16,128]{3,2,1,0:T(8,128)}, f32[3,8,16,128]{3,2,1,0:T(8,128)S(1)}, u32[]{:S(2)}) %copy-start) | copy-done | bytes 196632
  35.5 0.0 copy-start.2
  35.5 0.6 %copy-done.2 = bf16[16,16,128]{2,1,0:T(8,128)(2,1)} copy-done((bf16[16,16,128]{2,1,0:T(8,128)(2,1)}, bf16[16,16,128]{2,1,0:T(8,128)(2,1)S(1)}, u32[]{:S(2)}) %copy-start.2) | copy-done | bytes 65560
  36.1 0.0 copy-start.7
  36.1 0.6 %copy-done.7 = f32[8,8,128]{2,1,0:T(8,128)} copy-done((f32[8,8,128]{2,1,0:T(8,128)}, f32[8,8,128]{2,1,0:T(8,128)S(1)}, u32[]{:S(2)}) %copy-start.7) | copy-done | bytes 32792
  36.7 10.1 %store.1 = (f32[3,8,16,128]{3,2,1,0:T(8,128)}, bf16[16,16,128]{2,1,0:T(8,128)(2,1)}, f32[8,8,128]{2,1,0:T(8,128)}) custom-call(f32[3,8,16,128]{3,2,1,0:T(8,128)} %copy-done, bf16[16,16,128]{2,1,0:T(8,128)(2,1)} %copy-done.2, f32[8,8,128]{2,1,0:T(8,128)} %copy-done.7), custom_call_target="tpu_custom_call" | custom-call | tf_op jit(solution)/shard_map/store/pallas_call | solution.py:597
Async XLA Ops:
  0.6 0.7 %copy-start.11 = (s32[1024]{0:T(1024)S(1)}, s32[1024]{0:T(1024)}, u32[]{:S(2)}) copy-start(s32[1024]{0:T(1024)} %param.12) | copy-start | bytes 12292
  1.3 0.9 %copy-start.1 = (f32[3,8,16,128]{3,2,1,0:T(8,128)S(1)}, f32[3,8,16,128]{3,2,1,0:T(8,128)}, u32[]{:S(2)}) copy-start(f32[3,8,16,128]{3,2,1,0:T(8,128)} %refs_0_.1) | copy-start | bytes 589828
  2.2 0.8 %copy-start.3 = (f32[8,16,128]{2,1,0:T(8,128)S(1)}, f32[8,16,128]{2,1,0:T(8,128)}, u32[]{:S(2)}) copy-start(f32[8,16,128]{2,1,0:T(8,128)} %refs_1_.1) | copy-start | bytes 196612
  3.1 0.8 %copy-start.4 = (bf16[16,16,128]{2,1,0:T(8,128)(2,1)S(1)}, bf16[16,16,128]{2,1,0:T(8,128)(2,1)}, u32[]{:S(2)}) copy-start(bf16[16,16,128]{2,1,0:T(8,128)(2,1)} %refs_3_.1) | copy-start | bytes 196612
  3.9 0.8 %copy-start.5 = (bf16[9,64,24]{1,2,0:T(8,128)(2,1)S(1)}, bf16[9,64,24]{1,2,0:T(8,128)(2,1)}, u32[]{:S(2)}) copy-start(bf16[9,64,24]{1,2,0:T(8,128)(2,1)} %param.13) | copy-start | bytes 82948
  4.7 0.8 %copy-start.6 = (bf16[9,16,64]{2,1,0:T(8,128)(2,1)S(1)}, bf16[9,16,64]{2,1,0:T(8,128)(2,1)}, u32[]{:S(2)}) copy-start(bf16[9,16,64]{2,1,0:T(8,128)(2,1)} %refs_7_.1) | copy-start | bytes 55300
  5.5 0.8 %copy-start.8 = (s32[8192]{0:T(1024)S(1)}, s32[8192]{0:T(1024)}, u32[]{:S(2)}) copy-start(s32[8192]{0:T(1024)} %param.17) | copy-start | bytes 98308
  6.3 0.7 %copy-start.9 = (bf16[64,64]{1,0:T(8,128)(2,1)S(1)}, bf16[64,64]{1,0:T(8,128)(2,1)}, u32[]{:S(2)}) copy-start(bf16[64,64]{1,0:T(8,128)(2,1)} %refs_6_.1) | copy-start | bytes 24580
  7.0 0.7 %copy-start.10 = (s32[16,128]{1,0:T(8,128)S(1)}, s32[16,128]{1,0:T(8,128)}, u32[]{:S(2)}) copy-start(s32[16,128]{1,0:T(8,128)} %refs_2_.1) | copy-start | bytes 24580
  34.8 0.7 %copy-start = (f32[3,8,16,128]{3,2,1,0:T(8,128)}, f32[3,8,16,128]{3,2,1,0:T(8,128)S(1)}, u32[]{:S(2)}) copy-start(f32[3,8,16,128]{3,2,1,0:T(8,128)S(1)} %get-tuple-element.9.refs_0_) | copy-start | bytes 589828
  35.5 0.6 %copy-start.2 = (bf16[16,16,128]{2,1,0:T(8,128)(2,1)}, bf16[16,16,128]{2,1,0:T(8,128)(2,1)S(1)}, u32[]{:S(2)}) copy-start(bf16[16,16,128]{2,1,0:T(8,128)(2,1)S(1)} %get-tuple-element.10.refs_1_) | copy-start | bytes 196612
  36.1 0.6 %copy-start.7 = (f32[8,8,128]{2,1,0:T(8,128)}, f32[8,8,128]{2,1,0:T(8,128)S(1)}, u32[]{:S(2)}) copy-start(f32[8,8,128]{2,1,0:T(8,128)S(1)} %get-tuple-element.11.refs_2_) | copy-start | bytes 98308

commit v4 on v3

--- a/solution.py
+++ b/solution.py
@@ -11,8 +11,8 @@
 MESH = pl.DeviceIdType.MESH
 F32 = jnp.float32
 BF16 = jnp.bfloat16
+GRANT = 62 * 1024 * 1024
 WIDE = 4
-VMEM = pl.BlockSpec(memory_space=pltpu.VMEM)
 HBM = pl.BlockSpec(memory_space=pltpu.HBM)
 ANY = pl.BlockSpec(memory_space=pl.ANY)
 
@@ -78,7 +78,7 @@
     state, closure, out,
     krow, klane, coriolis, north_g, south_g, cot, closing, north, south, sides, tops, rows, packed, partner_pick, picks, w_first, w_last, w_back, w_mix_t,
     f_a, f_b, h_a, h_b, ks_a, ks_b, g_own, wet2s, patches, slope1, slope2, hid1, hid2, hshift, gpatch, dmix, dfirst, table,
-    picked, got_lon, got_lat, chunk,
+    picked, got_lon, got_lat, chunk, state_out, closure_out, out_sem,
     row_send, row_recv, g_send, g_recv, side_send, side_recv, top_send, top_recv, out_sem1, in_sem1, out_sem2, in_sem2, out_sem3, in_sem3,
 ):
     lon = lax.axis_index("lon")
@@ -488,10 +488,14 @@
         for j in range(2):
             r = start // 128 + j
             closing[:, r, :] = wet2s[r] * tend[:, 128 * j : 128 * j + 128]
-    closure[...] = closing[...].astype(BF16)
+    closure_out[...] = closing[...].astype(BF16)
+    save_closure = pltpu.make_async_copy(closure_out, closure, out_sem.at[0])
+    save_closure.start()
     for row in range(count):
         for f in range(3):
-            state[f, :, row, :] = f_a[row + WIDE, f]
+            state_out[f, :, row, :] = f_a[row + WIDE, f]
+    save_state = pltpu.make_async_copy(state_out, state, out_sem.at[1])
+    save_state.start()
     for c, to in zip(first, lons):
         c.wait_send()
         share(picked.at[to], got_lon.at[to], out_sem1.at[to], in_sem1.at[to], (to, lat)).wait_recv()
@@ -506,10 +510,13 @@
     third = [share(chunk, out.at[lon], out_sem3.at[to], in_sem3.at[lon], (to, lat)) for to in lons]
     for c in third:
         c.start()
-    out[lon] = chunk[...]
+    save_chunk = pltpu.make_async_copy(chunk, out.at[lon], out_sem.at[2])
+    save_chunk.start()
     for c, to in zip(third, lons):
         c.wait_send()
         share(chunk, out.at[to], out_sem3.at[to], in_sem3.at[to], (to, lat)).wait_recv()
+    for save in (save_chunk, save_state, save_closure):
+        save.wait()
 
 
 def entry_place(index):
@@ -531,14 +538,6 @@
     row = jnp.where(index < 13824, row_f, jnp.where(index < 17920, row_m, row_l))
     lane = jnp.where(index < 13824, lane_f, jnp.where(index < 17920, lane_m, lane_l))
     return row, lane
-
-
-def store_kernel(*refs):
-    copies = [pltpu.make_async_copy(refs[i], refs[3 + i], refs[6].at[i]) for i in range(3)]
-    for copy in copies:
-        copy.start()
-    for copy in copies:
-        copy.wait()
 
 
 def on_device(
@@ -563,11 +562,11 @@
     outs = [
         sds((3, 8, count, 128), F32), sds((16, count, 128), BF16), sds((n_lon, depth, 128), F32),
     ]
-    results = pl.pallas_call(
+    state, closure, reduced = pl.pallas_call(
         functools.partial(kernel, n_lon, n_lat, scale),
         out_shape=outs,
         in_specs=[HBM] * 9,
-        out_specs=[VMEM] * 3,
+        out_specs=[ANY] * 3,
         scratch_shapes=[vmem(x.shape, x.dtype) for x in operands] + [
             dma((9,)), vmem((picks, 128), jnp.int32), vmem((picks, 128), jnp.int32), vmem((total, 128), F32),
             vmem((16, 128), BF16), vmem((16, 128), BF16),
@@ -585,23 +584,15 @@
             vmem((144, cells), BF16), vmem((64, cells), BF16), vmem((64, cells), BF16),
             vmem((256, 128), F32),
             vmem((n_lon, depth, 128), F32), vmem((n_lon, depth, 128), F32), vmem((n_lat, depth, 128), F32),
-            vmem((depth, 128), F32),
+            vmem((depth, 128), F32), vmem((3, 8, count, 128), F32), vmem((16, count, 128), BF16), dma((3,)),
             dma((2,)), dma((2,)), dma((2,)), dma((2,)), dma((6,)), dma((6,)), dma((n_lon,)), dma((n_lon,)),
             dma((n_lon,)), dma((n_lon,)), dma((n_lat,)), dma((n_lat,)), dma((n_lon,)), dma((n_lon,)),
         ],
         compiler_params=pltpu.CompilerParams(
-            collective_id=0, has_side_effects=True, vmem_limit_bytes=48 * 1024 * 1024
+            collective_id=0, has_side_effects=True, vmem_limit_bytes=GRANT
         ),
         name="ocean",
     )(*operands)
-    state, closure, reduced = pl.pallas_call(
-        store_kernel,
-        out_shape=outs,
-        in_specs=[ANY] * 3,
-        out_specs=[ANY] * 3,
-        scratch_shapes=[dma((3,))],
-        name="store",
-    )(*results)
     return state, closure, reduced.reshape(-1)
 
 

time: 47.3 us -> 30.6 us (0.65)
  Pallas kernels: 37.2 us -> 26.7 us
  local copies, waits for them, and re-layouts: 8.92 us -> 3.03 us
    pallas_call x1 -> x0, Pallas kernels: 10.1 us -> none  [on_device(): pl.pallas_call(store_kernel, out_shape=outs, in_specs=[ANY] * 3, out_spec...]
    unnamed x24 -> x7, local copies, waits for them, and re-layouts: 8.92 us -> 3.03 us
where the time goes in v4:
time: 30.6 us; the launch traced here: 30.4 us
  Pallas kernels  26.7 us (87%)
  local copies, waits for them, and re-layouts  3.03 us (10%)
  between operations  0.65 us (2%)
    pallas_call x1, Pallas kernels, on_device(): pl.pallas_call(functools.partial(kernel, n_lon, n_lat, scale), out_shape=...  26.7 us
    unnamed x7, local copies, waits for them, and re-layouts  3.03 us

profile of v4, /device:TPU:0, one launch (start us, length us, event | category | flops | bytes accessed | tf_op | source)
XLA Modules:
  0.0 30.4 jit_solution(10975825789875500162)
XLA Ops:
  0.6 26.7 %ocean.1 = (f32[3,8,16,128]{3,2,1,0:T(8,128)}, bf16[16,16,128]{2,1,0:T(8,128)(2,1)}, f32[8,8,128]{2,1,0:T(8,128)}) custom-call(f32[3,8,16,128]{3,2,1,0:T(8,128)} %refs_0_.1, f32[8,16,128]{2,1,0:T(8,128)} %refs_1_.1, s32[16,128]{1,0:T(8,128)} %refs_2_.1, bf16[16,16,128]{2,1,0:T(8,128)(2,1)} %refs_3_.1, s32[8,128]{1,0:T(8,128)} %bitcast.7, ...), custom_call_target="tpu_custom_call" | custom-call | tf_op jit(solution)/shard_map/ocean/pallas_call | solution.py:565
  27.3 0.0 copy-start
  27.4 1.6 %copy.15 = f32[3,8,16,128]{3,2,1,0:T(8,128)} copy(f32[3,8,16,128]{3,2,1,0:T(8,128)} %get-tuple-element.12) | data formatting | bytes 393216
  29.0 0.0 copy-done
  29.0 0.0 copy-start.1
  29.0 0.6 %copy.16 = bf16[16,16,128]{2,1,0:T(8,128)(2,1)} copy(bf16[16,16,128]{2,1,0:T(8,128)(2,1)S(1)} %copy-done) | data formatting | bytes 131072
  29.6 0.1 copy-done.1
  29.8 0.6 %copy.17 = f32[8192]{0:T(1024)} copy(f32[8192]{0:T(1024)S(1)} %bitcast.5) | data formatting | bytes 65536
Async XLA Ops:
  27.3 1.7 %copy-start = (bf16[16,16,128]{2,1,0:T(8,128)(2,1)S(1)}, bf16[16,16,128]{2,1,0:T(8,128)(2,1)}, u32[]{:S(2)}) copy-start(bf16[16,16,128]{2,1,0:T(8,128)(2,1)} %get-tuple-element.13) | copy-start | bytes 196612
  29.0 0.8 %copy-start.1 = (f32[8,8,128]{2,1,0:T(8,128)S(1)}, f32[8,8,128]{2,1,0:T(8,128)}, u32[]{:S(2)}) copy-start(f32[8,8,128]{2,1,0:T(8,128)} %get-tuple-element.8) | copy-start | bytes 98308

commit v5 on v4

--- a/solution.py
+++ b/solution.py
@@ -315,8 +315,8 @@
     for row in range(count):
         put(row + WIDE, None, unpack(mid, row))
     low, high = WIDE, WIDE + count - 1
-    lax.fori_loop(low, high, roots, 0, unroll=3)
-    lax.fori_loop(low + 1, high, first_step, 0, unroll=2)
+    lax.fori_loop(low, high, roots, 0, unroll=5)
+    lax.fori_loop(low + 1, high, first_step, 0, unroll=7)
 
     @pl.when(has_north)
     def _():
@@ -371,9 +371,9 @@
 
     lax.fori_loop(0, low, roots, 0, unroll=True)
     lax.fori_loop(high, total - 1, roots, 0, unroll=True)
-    lax.fori_loop(1, low + 1, first_step, 0, unroll=2)
-    lax.fori_loop(high, total - 1, first_step, 0, unroll=2)
-    lax.fori_loop(2, total - 2, step(h_a, h_b, f_a, f_b), 0, unroll=2)
+    lax.fori_loop(1, low + 1, first_step, 0, unroll=True)
+    lax.fori_loop(high, total - 1, first_step, 0, unroll=True)
+    lax.fori_loop(2, total - 2, step(h_a, h_b, f_a, f_b), 0, unroll=5)
 
     lane24 = lax.broadcasted_iota(jnp.int32, (24, 128), 1)
     lane72 = lax.broadcasted_iota(jnp.int32, (72, 128), 1)

time: 30.6 us -> 29.9 us (0.977)
  Pallas kernels: 26.7 us -> 26 us
    pallas_call x1, Pallas kernels: 26.7 us -> 26 us  [on_device(): pl.pallas_call(functools.partial(kernel, n_lon, n_lat, scale), out_shape=...]
where the time goes in v5:
time: 29.9 us; the launch traced here: 29.7 us
  Pallas kernels  26 us (87%)
  local copies, waits for them, and re-layouts  3.03 us (10%)
  between operations  0.65 us (2%)
    pallas_call x1, Pallas kernels, on_device(): pl.pallas_call(functools.partial(kernel, n_lon, n_lat, scale), out_shape=...  26 us
    unnamed x7, local copies, waits for them, and re-layouts  3.03 us

profile of v5, /device:TPU:0, one launch (start us, length us, event | category | flops | bytes accessed | tf_op | source)
XLA Modules:
  0.0 29.7 jit_solution(9572002561284636821)
XLA Ops:
  0.6 26.0 %ocean.1 = (f32[3,8,16,128]{3,2,1,0:T(8,128)}, bf16[16,16,128]{2,1,0:T(8,128)(2,1)}, f32[8,8,128]{2,1,0:T(8,128)}) custom-call(f32[3,8,16,128]{3,2,1,0:T(8,128)} %refs_0_.1, f32[8,16,128]{2,1,0:T(8,128)} %refs_1_.1, s32[16,128]{1,0:T(8,128)} %refs_2_.1, bf16[16,16,128]{2,1,0:T(8,128)(2,1)} %refs_3_.1, s32[8,128]{1,0:T(8,128)} %bitcast.7, ...), custom_call_target="tpu_custom_call" | custom-call | tf_op jit(solution)/shard_map/ocean/pallas_call | solution.py:565
  26.6 0.0 copy-start
  26.6 1.6 %copy.15 = f32[3,8,16,128]{3,2,1,0:T(8,128)} copy(f32[3,8,16,128]{3,2,1,0:T(8,128)} %get-tuple-element.12) | data formatting | bytes 393216
  28.3 0.0 copy-done
  28.3 0.0 copy-start.1
  28.3 0.6 %copy.16 = bf16[16,16,128]{2,1,0:T(8,128)(2,1)} copy(bf16[16,16,128]{2,1,0:T(8,128)(2,1)S(1)} %copy-done) | data formatting | bytes 131072
  28.9 0.1 copy-done.1
  29.0 0.6 %copy.17 = f32[8192]{0:T(1024)} copy(f32[8192]{0:T(1024)S(1)} %bitcast.5) | data formatting | bytes 65536
Async XLA Ops:
  26.6 1.7 %copy-start = (bf16[16,16,128]{2,1,0:T(8,128)(2,1)S(1)}, bf16[16,16,128]{2,1,0:T(8,128)(2,1)}, u32[]{:S(2)}) copy-start(bf16[16,16,128]{2,1,0:T(8,128)(2,1)} %get-tuple-element.13) | copy-start | bytes 196612
  28.3 0.8 %copy-start.1 = (f32[8,8,128]{2,1,0:T(8,128)S(1)}, f32[8,8,128]{2,1,0:T(8,128)}, u32[]{:S(2)}) copy-start(f32[8,8,128]{2,1,0:T(8,128)} %get-tuple-element.8) | copy-start | bytes 98308
